TPU v7x, 32 devices: a whole 2x2x4 slice. The times are simulated.
32 devices in a mesh: row: 8 (over y, x, core), col: 4 (over z).
Axes of the slice: x: 2, y: 2, z: 4, core: 2. Of those that a mesh axis runs over, the one named last changes fastest.
Arguments:
- covariance: float32 [12288, 12288], P('row', 'col'), may hold values from -6 to 6
- east_wind: float32 [96, 128], replicated, may hold values from -0.3 to 0.3
- north_wind: float32 [96, 128], replicated, may hold values from -0.3 to 0.3
- diffuse_lon: float32 [96, 128], replicated, may hold values from 0.05 to 0.2
- diffuse_lat: float32 [96, 128], replicated, may hold values from 0.05 to 0.2
Outputs:
- propagated: float32 [12288, 12288], P('row', 'col')
All inputs are finite; a program needn't handle non-finite values.
Results may differ from a plain program's by a relative error of at most 0.00002.
Values sent between devices are 32-bit elements; how exact they have to be, the bound alone decides.
A program may use at most 192 MiB of HBM per device.

v0:
```python
import jax
import jax.numpy as jnp
from jax import lax
from jax.sharding import PartitionSpec as P

NLON = 128
STEPS = 3


def extended(shard, sides, width):
    for axis, dim in sides:
        devices, length = (lax.axis_size(axis), shard.shape[dim])
        up = [(i, (i + 1) % devices) for i in range(devices - 1)]
        down = [(j, i) for i, j in up]
        last = lax.slice_in_dim(shard, length - width, length, axis=dim)
        first = lax.slice_in_dim(shard, 0, width, axis=dim)
        before = lax.ppermute(last, axis, up)
        after = lax.ppermute(first, axis, down)
        shard = jnp.concatenate([before, shard, after], axis=dim)
    return shard


def advect(widened, lat_dim, east_wind, north_wind, diffuse_lon, diffuse_lat):
    length = widened.shape[lat_dim]
    north = lax.slice_in_dim(widened, 2, length, axis=lat_dim)
    south = lax.slice_in_dim(widened, 0, length - 2, axis=lat_dim)
    center = lax.slice_in_dim(widened, 1, length - 1, axis=lat_dim)
    eastern = jnp.roll(center, -1, lat_dim + 1)
    western = jnp.roll(center, 1, lat_dim + 1)
    return (
        center
        - 0.5 * east_wind * (eastern - western)
        - 0.5 * north_wind * (north - south)
        + diffuse_lon * (eastern - 2.0 * center + western)
        + diffuse_lat * (north - 2.0 * center + south)
    )


def shaped(table, lat_dim, rank):
    return table.reshape([1] * lat_dim + list(table.shape) + [1] * (rank - lat_dim - 2))


def sweep(values, lat_dim, offset, tables):
    lines = values.shape[lat_dim]
    local = [shaped(lax.dynamic_slice_in_dim(t, offset, lines, 0), lat_dim, 3) for t in tables]
    for section in range(STEPS):
        if lat_dim == 0:
            widened = extended(values, (("row", 0),), 1)
        else:
            widened = extended(values, (("col", 1),), 1)
        values = advect(widened, lat_dim, *local)
    return values


def body(covariance, east_wind, north_wind, diffuse_lon, diffuse_lat):
    tables = (east_wind, north_wind, diffuse_lon, diffuse_lat)
    rows_here, cols_here = covariance.shape
    row_lines = rows_here // NLON
    col_lines = cols_here // NLON
    row_offset = lax.axis_index("row") * row_lines
    col_offset = lax.axis_index("col") * col_lines
    values = covariance.reshape(row_lines, NLON, cols_here)
    values = sweep(values, 0, row_offset, tables)
    values = values.reshape(rows_here, col_lines, NLON)
    values = sweep(values, 1, col_offset, tables)
    return values.reshape(rows_here, cols_here)


def solution(mesh):
    return jax.shard_map(
        body,
        mesh=mesh,
        in_specs=(P("row", "col"), P(), P(), P(), P()),
        out_specs=P("row", "col"),
        check_vma=False,
    )
```

profile of v0, /device:TPU:10, one launch (start us, length us, event | category | flops | bytes accessed | tf_op | source)
XLA Modules:
  0.0 579.1 jit_solution(13217914699763837620)
XLA Ops:
  0.0 2.1 slice_bitcast_fusion
  2.1 1.9 collective-permute-start.1
  4.0 3.6 collective-permute-start
  7.7 0.7 dynamic-slice_multiply_fusion.2
  8.4 1.3 dynamic-slice_multiply_fusion
  9.8 0.7 constant_dynamic-slice_fusion.2
  10.5 1.3 constant_dynamic-slice_fusion
  11.8 1.8 fusion.16
  13.6 26.2 %fusion.15 = (f32[12,127,3072]{2,1,0:T(8,128)}, f32[12,127,3072]{2,1,0:T(8,128)}) fusion(f32[12,128,3072]{2,1,0:T(8,128)} %bitcast.21), kind=kLoop, calls=%fused_computation.56 | loop fusion | bytes 74907648 | tf_op jit(solution)/shard_map/jit(_roll_static)/slice | solution.py:28
  39.9 38.3 %multiply_add_fusion.5 = f32[12,128,3072]{2,1,0:T(8,128)} fusion(f32[12,128,3072]{2,1,0:T(8,128)} %bitcast.22, f32[1,128,3072]{2,1,0:T(8,128)} %collective-permute-done, f32[1,128,3072]{2,1,0:T(8,128)} %collective-permute-done.1, f32[12,127,3072]{2,1,0:T(8,128)} %get-tuple-element.36, f32[12,1,3072]{2,1,0:T(1,128)S(1)} %get-tuple-element.38, ...), kind=kLoop, calls=%fused_computation.30 | loop fusion | flops 89653248 | bytes 78667776 | tf_op jit(solution)/shard_map/add | solution.py:31
  78.2 1.8 fusion.13
  80.1 2.1 fusion.14
  82.2 3.6 collective-permute-start.3
  85.7 2.1 collective-permute-start.2
  87.8 26.0 %fusion.12 = (f32[12,127,3072]{2,1,0:T(8,128)}, f32[12,127,3072]{2,1,0:T(8,128)}) fusion(f32[12,128,3072]{2,1,0:T(8,128)} %multiply_add_fusion.5), kind=kLoop, calls=%fused_computation.53 | loop fusion | bytes 74907648 | tf_op jit(solution)/shard_map/jit(_roll_static)/slice | solution.py:28
  113.8 6.9 %collective-permute-done.2 = f32[1,128,3072]{2,1,0:T(8,128)S(1)} collective-permute-done((f32[1,128,3072]{2,1,0:T(8,128)S(1)}, f32[1,128,3072]{2,1,0:T(8,128)S(1)}, u32[]{:S(2)}, u32[]{:S(2)}) %collective-permute-start.2) | collective-permute-done | bytes 1572896 | tf_op jit(solution)/shard_map/ppermute | solution.py:18
  120.7 38.4 %multiply_add_fusion.4 = f32[12,128,3072]{2,1,0:T(8,128)} fusion(f32[12,128,3072]{2,1,0:T(8,128)} %multiply_add_fusion.5, f32[1,128,3072]{2,1,0:T(8,128)S(1)} %collective-permute-done.2, f32[1,128,3072]{2,1,0:T(8,128)S(1)} %collective-permute-done.3, f32[12,127,3072]{2,1,0:T(8,128)} %get-tuple-element.30, f32[12,1,3072]{2,1,0:T(1,128)S(1)} %get-tuple-element.32, ...), kind=kLoop, calls=%fused_computation.29 | loop fusion | flops 89653248 | bytes 78667776 | tf_op jit(solution)/shard_map/add | solution.py:31
  159.1 1.8 fusion.10
  160.9 2.1 fusion.11
  163.0 2.8 collective-permute-start.5
  165.8 3.5 collective-permute-start.4
  169.3 26.1 %fusion.9 = (f32[12,127,3072]{2,1,0:T(8,128)}, f32[12,127,3072]{2,1,0:T(8,128)}) fusion(f32[12,128,3072]{2,1,0:T(8,128)} %multiply_add_fusion.4), kind=kLoop, calls=%fused_computation.50 | loop fusion | bytes 74907648 | tf_op jit(solution)/shard_map/jit(_roll_static)/slice | solution.py:28
  195.4 0.0 collective-permute-done.5
  195.4 5.1 collective-permute-done.4
  200.5 38.6 %multiply_add_fusion.3 = f32[12,128,3072]{2,1,0:T(8,128)} fusion(f32[12,128,3072]{2,1,0:T(8,128)} %multiply_add_fusion.4, f32[1,128,3072]{2,1,0:T(8,128)S(1)} %collective-permute-done.4, f32[1,128,3072]{2,1,0:T(8,128)S(1)} %collective-permute-done.5, f32[12,127,3072]{2,1,0:T(8,128)} %get-tuple-element.24, f32[12,1,3072]{2,1,0:T(1,128)S(1)} %get-tuple-element.26, ...), kind=kLoop, calls=%fused_computation.28 | loop fusion | flops 89653248 | bytes 78667776 | tf_op jit(solution)/shard_map/add | solution.py:31
  239.1 10.3 %copy.6 = f32[192,8,24,128]{3,2,1,0:T(8,128)S(1)} copy(f32[192,8,24,128]{3,1,2,0:T(8,128)} %bitcast.23) | data formatting | bytes 37748736
  249.4 0.0 copy-start
  249.4 1.1 fusion.8
  250.6 15.5 %fusion.7 = (f32[1536,24,1]{2,1,0:T(8,128)}, f32[1536,24,1]{2,1,0:T(8,128)}) fusion(f32[1536,24,128]{2,1,0:T(8,128)S(1)} %bitcast.17), kind=kLoop, calls=%fused_computation.48 | loop fusion | bytes 589824 | tf_op jit(solution)/shard_map/jit(_roll_static)/slice | solution.py:28
  266.1 3.5 collective-permute-start.7
  269.6 2.7 collective-permute-start.6
  272.3 13.3 %fusion.6 = (f32[1536,24,127]{2,1,0:T(8,128)}, f32[1536,24,127]{2,1,0:T(8,128)}) fusion(f32[1536,24,128]{2,1,0:T(8,128)S(1)} %bitcast.18), kind=kLoop, calls=%fused_computation.47 | loop fusion | bytes 74907648 | tf_op jit(solution)/shard_map/jit(_roll_static)/slice | solution.py:28
  285.7 2.5 collective-permute-done.6
  288.1 54.0 %multiply_add_fusion.2 = f32[1536,24,128]{2,1,0:T(8,128)} fusion(f32[1536,24,128]{2,1,0:T(8,128)} %bitcast.19, f32[1536,1,128]{2,1,0:T(1,128)S(1)} %collective-permute-done.6, f32[1536,1,128]{2,1,0:T(1,128)S(1)} %collective-permute-done.7, f32[1536,24,127]{2,1,0:T(8,128)} %get-tuple-element.18, f32[1536,24,1]{2,1,0:T(8,128)} %get-tuple-element.20, ...), kind=kLoop, calls=%fused_computation.27 | loop fusion | flops 89653248 | bytes 77119488 | tf_op jit(solution)/shard_map/add | solution.py:31
  342.1 5.4 fusion.5
  347.6 30.7 %fusion.4 = (f32[1536,24,1]{2,1,0:T(8,128)}, f32[1536,24,1]{2,1,0:T(8,128)}) fusion(f32[1536,24,128]{2,1,0:T(8,128)} %multiply_add_fusion.2), kind=kLoop, calls=%fused_computation.45 | loop fusion | bytes 589824 | tf_op jit(solution)/shard_map/jit(_roll_static)/slice | solution.py:28
  378.2 3.5 collective-permute-start.9
  381.7 2.6 collective-permute-start.8
  384.4 13.6 %fusion.3 = (f32[1536,24,127]{2,1,0:T(8,128)}, f32[1536,24,127]{2,1,0:T(8,128)}) fusion(f32[1536,24,128]{2,1,0:T(8,128)S(1)} %bitcast.15), kind=kLoop, calls=%fused_computation.44 | loop fusion | bytes 74907648 | tf_op jit(solution)/shard_map/jit(_roll_static)/slice | solution.py:28
  398.0 0.9 collective-permute-done.8
  398.9 53.1 %multiply_add_fusion.1 = f32[1536,24,128]{2,1,0:T(8,128)} fusion(f32[1536,24,128]{2,1,0:T(8,128)} %multiply_add_fusion.2, f32[1536,1,128]{2,1,0:T(1,128)S(1)} %collective-permute-done.8, f32[1536,1,128]{2,1,0:T(1,128)S(1)} %collective-permute-done.9, f32[1536,24,127]{2,1,0:T(8,128)} %get-tuple-element.12, f32[1536,24,1]{2,1,0:T(8,128)} %get-tuple-element.14, ...), kind=kLoop, calls=%fused_computation.26 | loop fusion | flops 89653248 | bytes 77119488 | tf_op jit(solution)/shard_map/add | solution.py:31
  452.0 5.5 fusion.2
  457.5 30.7 %fusion.1 = (f32[1536,24,1]{2,1,0:T(8,128)}, f32[1536,24,1]{2,1,0:T(8,128)}) fusion(f32[1536,24,128]{2,1,0:T(8,128)} %multiply_add_fusion.1), kind=kLoop, calls=%fused_computation.42 | loop fusion | bytes 589824 | tf_op jit(solution)/shard_map/jit(_roll_static)/slice | solution.py:28
  488.2 2.5 collective-permute-start.11
  490.7 3.6 collective-permute-start.10
  494.4 13.6 %fusion = (f32[1536,24,127]{2,1,0:T(8,128)}, f32[1536,24,127]{2,1,0:T(8,128)}) fusion(f32[1536,24,128]{2,1,0:T(8,128)S(1)} %bitcast.13), kind=kLoop, calls=%fused_computation.41 | loop fusion | bytes 74907648 | tf_op jit(solution)/shard_map/jit(_roll_static)/slice | solution.py:28
  508.0 53.0 %multiply_add_fusion = f32[1536,24,128]{2,1,0:T(8,128)} fusion(f32[1536,24,128]{2,1,0:T(8,128)} %multiply_add_fusion.1, f32[1536,1,128]{2,1,0:T(1,128)S(1)} %collective-permute-done.10, f32[1536,1,128]{2,1,0:T(1,128)S(1)} %collective-permute-done.11, f32[1536,24,127]{2,1,0:T(8,128)} %get-tuple-element.6, f32[1536,24,1]{2,1,0:T(8,128)} %get-tuple-element.8, ...), kind=kLoop, calls=%fused_computation.25 | loop fusion | flops 89653248 | bytes 77119488 | tf_op jit(solution)/shard_map/add | solution.py:31
  561.0 17.8 %copy.9 = f32[192,8,24,128]{3,1,2,0:T(8,128)} copy(f32[192,8,24,128]{3,2,1,0:T(8,128)} %bitcast.24) | data formatting | bytes 37748736
  (38 shorter events, 0.1 us)
Async XLA Ops:
  2.1 37.8 %collective-permute-start.1 = (f32[1,128,3072]{2,1,0:T(8,128)S(1)}, f32[1,128,3072]{2,1,0:T(8,128)}, u32[]{:S(2)}, u32[]{:S(2)}) collective-permute-start(f32[1,128,3072]{2,1,0:T(8,128)S(1)} %get-tuple-element.39), channel_id=1, source_target_pairs={{0,4},{4,8},{8,12},{12,16},{16,20},{20,24},{24,28},{1,5},{5,9},{9,... | collective-permute-start | bytes 4718600 | tf_op jit(solution)/shard_map/ppermute | solution.py:17
  4.0 35.9 %collective-permute-start = (f32[1,128,3072]{2,1,0:T(8,128)S(1)}, f32[1,128,3072]{2,1,0:T(8,128)}, u32[]{:S(2)}, u32[]{:S(2)}) collective-permute-start(f32[1,128,3072]{2,1,0:T(8,128)S(1)} %get-tuple-element.40), channel_id=1, source_target_pairs={{4,0},{8,4},{12,8},{16,12},{20,16},{24,20},{28,24},{5,1},{9,5},{13... | collective-permute-start | bytes 4718600 | tf_op jit(solution)/shard_map/ppermute | solution.py:18
  82.2 31.6 %collective-permute-start.3 = (f32[1,128,3072]{2,1,0:T(8,128)S(1)}, f32[1,128,3072]{2,1,0:T(8,128)S(1)}, u32[]{:S(2)}, u32[]{:S(2)}) collective-permute-start(f32[1,128,3072]{2,1,0:T(8,128)S(1)} %get-tuple-element.33), channel_id=1, source_target_pairs={{0,4},{4,8},{8,12},{12,16},{16,20},{20,24},{24,28},{1,5},{5,9},{9,... | collective-permute-start | bytes 4718600 | tf_op jit(solution)/shard_map/ppermute | solution.py:17
  85.7 34.9 %collective-permute-start.2 = (f32[1,128,3072]{2,1,0:T(8,128)S(1)}, f32[1,128,3072]{2,1,0:T(8,128)S(1)}, u32[]{:S(2)}, u32[]{:S(2)}) collective-permute-start(f32[1,128,3072]{2,1,0:T(8,128)S(1)} %get-tuple-element.34), channel_id=1, source_target_pairs={{4,0},{8,4},{12,8},{16,12},{20,16},{24,20},{28,24},{5,1},{9,5},{13... | collective-permute-start | bytes 4718600 | tf_op jit(solution)/shard_map/ppermute | solution.py:18
  163.0 32.4 %collective-permute-start.5 = (f32[1,128,3072]{2,1,0:T(8,128)S(1)}, f32[1,128,3072]{2,1,0:T(8,128)S(1)}, u32[]{:S(2)}, u32[]{:S(2)}) collective-permute-start(f32[1,128,3072]{2,1,0:T(8,128)S(1)} %get-tuple-element.27), channel_id=1, source_target_pairs={{0,4},{4,8},{8,12},{12,16},{16,20},{20,24},{24,28},{1,5},{5,9},{9,... | collective-permute-start | bytes 4718600 | tf_op jit(solution)/shard_map/ppermute | solution.py:17
  165.8 34.7 %collective-permute-start.4 = (f32[1,128,3072]{2,1,0:T(8,128)S(1)}, f32[1,128,3072]{2,1,0:T(8,128)S(1)}, u32[]{:S(2)}, u32[]{:S(2)}) collective-permute-start(f32[1,128,3072]{2,1,0:T(8,128)S(1)} %get-tuple-element.28), channel_id=1, source_target_pairs={{4,0},{8,4},{12,8},{16,12},{20,16},{24,20},{28,24},{5,1},{9,5},{13... | collective-permute-start | bytes 4718600 | tf_op jit(solution)/shard_map/ppermute | solution.py:18
  249.4 22.9 %copy-start = (f32[192,8,24,128]{3,2,1,0:T(8,128)}, f32[192,8,24,128]{3,2,1,0:T(8,128)S(1)}, u32[]{:S(2)}) copy-start(f32[192,8,24,128]{3,2,1,0:T(8,128)S(1)} %copy.6) | copy-start | bytes 56623108
  266.1 19.6 %collective-permute-start.7 = (f32[1536,1,128]{2,1,0:T(1,128)S(1)}, f32[1536,1,128]{2,1,0:T(1,128)S(1)}, u32[]{:S(2)}, u32[]{:S(2)}) collective-permute-start(f32[1536,1,128]{2,1,0:T(1,128)S(1)} %get-tuple-element.21), channel_id=1, source_target_pairs={{0,1},{1,2},{2,3},{4,5},{5,6},{6,7},{8,9},{9,10},{10,11},{12,13},{... | collective-permute-start | bytes 2359304 | tf_op jit(solution)/shard_map/ppermute | solution.py:17
  269.6 18.6 %copy-start.1 = (f32[24,128]{1,0:T(8,128)S(1)}, f32[24,128]{1,0:T(8,128)}, u32[]{:S(2)}) copy-start(f32[24,128]{1,0:T(8,128)} %get-tuple-element.45) | copy-start | bytes 36868
  269.6 18.6 %copy-start.2 = (f32[24,128]{1,0:T(8,128)S(1)}, f32[24,128]{1,0:T(8,128)}, u32[]{:S(2)}) copy-start(f32[24,128]{1,0:T(8,128)} %get-tuple-element.46) | copy-start | bytes 36868
  269.6 18.6 %copy-start.3 = (f32[24,128]{1,0:T(8,128)S(1)}, f32[24,128]{1,0:T(8,128)}, u32[]{:S(2)}) copy-start(f32[24,128]{1,0:T(8,128)} %get-tuple-element.47) | copy-start | bytes 36868
  269.6 18.5 %copy-start.4 = (f32[24,128]{1,0:T(8,128)S(1)}, f32[24,128]{1,0:T(8,128)}, u32[]{:S(2)}) copy-start(f32[24,128]{1,0:T(8,128)} %get-tuple-element.48) | copy-start | bytes 36868
  269.6 18.5 %collective-permute-start.6 = (f32[1536,1,128]{2,1,0:T(1,128)S(1)}, f32[1536,1,128]{2,1,0:T(1,128)S(1)}, u32[]{:S(2)}, u32[]{:S(2)}) collective-permute-start(f32[1536,1,128]{2,1,0:T(1,128)S(1)} %get-tuple-element.22), channel_id=1, source_target_pairs={{1,0},{2,1},{3,2},{5,4},{6,5},{7,6},{9,8},{10,9},{11,10},{13,12},{... | collective-permute-start | bytes 2359304 | tf_op jit(solution)/shard_map/ppermute | solution.py:18
  342.1 42.2 %slice-start.5 = ((s8[18874368]{0:T(1024)(128)(4,1)}), s8[4194304]{0:T(1024)(128)(4,1)S(1)}, s32[]{:S(2)}) async-start(s8[18874368]{0:T(1024)(128)(4,1)} %bitcast.14), calls=%async_computation.5 | async-start | bytes 8388608
  347.5 36.8 %slice-start.6 = ((s8[18874368]{0:T(1024)(128)(4,1)}), s8[4194304]{0:T(1024)(128)(4,1)S(1)}, s32[]{:S(2)}) async-start(s8[18874368]{0:T(1024)(128)(4,1)} %bitcast.14), calls=%async_computation.6 | async-start | bytes 8388608
  347.5 36.8 %slice-start.7 = ((s8[18874368]{0:T(1024)(128)(4,1)}), s8[4194304]{0:T(1024)(128)(4,1)S(1)}, s32[]{:S(2)}) async-start(s8[18874368]{0:T(1024)(128)(4,1)} %bitcast.14), calls=%async_computation.7 | async-start | bytes 8388608
  347.5 36.8 %slice-start.8 = ((s8[18874368]{0:T(1024)(128)(4,1)}), s8[4194304]{0:T(1024)(128)(4,1)S(1)}, s32[]{:S(2)}) async-start(s8[18874368]{0:T(1024)(128)(4,1)} %bitcast.14), calls=%async_computation.8 | async-start | bytes 8388608
  347.6 36.8 %slice-start.9 = ((s8[18874368]{0:T(1024)(128)(4,1)}), s8[2097152]{0:T(1024)(128)(4,1)S(1)}, s32[]{:S(2)}) async-start(s8[18874368]{0:T(1024)(128)(4,1)} %bitcast.14), calls=%async_computation.9 | async-start | bytes 4194304
  378.2 19.7 %collective-permute-start.9 = (f32[1536,1,128]{2,1,0:T(1,128)S(1)}, f32[1536,1,128]{2,1,0:T(1,128)S(1)}, u32[]{:S(2)}, u32[]{:S(2)}) collective-permute-start(f32[1536,1,128]{2,1,0:T(1,128)S(1)} %get-tuple-element.15), channel_id=1, source_target_pairs={{0,1},{1,2},{2,3},{4,5},{5,6},{6,7},{8,9},{9,10},{10,11},{12,13},{... | collective-permute-start | bytes 2359304 | tf_op jit(solution)/shard_map/ppermute | solution.py:17
  381.7 17.2 %collective-permute-start.8 = (f32[1536,1,128]{2,1,0:T(1,128)S(1)}, f32[1536,1,128]{2,1,0:T(1,128)S(1)}, u32[]{:S(2)}, u32[]{:S(2)}) collective-permute-start(f32[1536,1,128]{2,1,0:T(1,128)S(1)} %get-tuple-element.16), channel_id=1, source_target_pairs={{1,0},{2,1},{3,2},{5,4},{6,5},{7,6},{9,8},{10,9},{11,10},{13,12},{... | collective-permute-start | bytes 2359304 | tf_op jit(solution)/shard_map/ppermute | solution.py:18
  452.0 42.3 %slice-start = ((s8[18874368]{0:T(1024)(128)(4,1)}), s8[4194304]{0:T(1024)(128)(4,1)S(1)}, s32[]{:S(2)}) async-start(s8[18874368]{0:T(1024)(128)(4,1)} %bitcast.12), calls=%async_computation | async-start | bytes 8388608
  457.5 36.9 %slice-start.1 = ((s8[18874368]{0:T(1024)(128)(4,1)}), s8[4194304]{0:T(1024)(128)(4,1)S(1)}, s32[]{:S(2)}) async-start(s8[18874368]{0:T(1024)(128)(4,1)} %bitcast.12), calls=%async_computation.1 | async-start | bytes 8388608
  457.5 36.9 %slice-start.2 = ((s8[18874368]{0:T(1024)(128)(4,1)}), s8[4194304]{0:T(1024)(128)(4,1)S(1)}, s32[]{:S(2)}) async-start(s8[18874368]{0:T(1024)(128)(4,1)} %bitcast.12), calls=%async_computation.2 | async-start | bytes 8388608
  457.5 36.9 %slice-start.3 = ((s8[18874368]{0:T(1024)(128)(4,1)}), s8[4194304]{0:T(1024)(128)(4,1)S(1)}, s32[]{:S(2)}) async-start(s8[18874368]{0:T(1024)(128)(4,1)} %bitcast.12), calls=%async_computation.3 | async-start | bytes 8388608
  457.5 36.9 %slice-start.4 = ((s8[18874368]{0:T(1024)(128)(4,1)}), s8[2097152]{0:T(1024)(128)(4,1)S(1)}, s32[]{:S(2)}) async-start(s8[18874368]{0:T(1024)(128)(4,1)} %bitcast.12), calls=%async_computation.4 | async-start | bytes 4194304
  488.2 19.8 %collective-permute-start.11 = (f32[1536,1,128]{2,1,0:T(1,128)S(1)}, f32[1536,1,128]{2,1,0:T(1,128)S(1)}, u32[]{:S(2)}, u32[]{:S(2)}) collective-permute-start(f32[1536,1,128]{2,1,0:T(1,128)S(1)} %get-tuple-element.9), channel_id=1, source_target_pairs={{0,1},{1,2},{2,3},{4,5},{5,6},{6,7},{8,9},{9,10},{10,11},{12,13},{... | collective-permute-start | bytes 2359304 | tf_op jit(solution)/shard_map/ppermute | solution.py:17
  490.7 17.3 %collective-permute-start.10 = (f32[1536,1,128]{2,1,0:T(1,128)S(1)}, f32[1536,1,128]{2,1,0:T(1,128)S(1)}, u32[]{:S(2)}, u32[]{:S(2)}) collective-permute-start(f32[1536,1,128]{2,1,0:T(1,128)S(1)} %get-tuple-element.10), channel_id=1, source_target_pairs={{1,0},{2,1},{3,2},{5,4},{6,5},{7,6},{9,8},{10,9},{11,10},{13,12},{... | collective-permute-start | bytes 2359304 | tf_op jit(solution)/shard_map/ppermute | solution.py:18
where the time goes:
time: 588 us; the launch traced here: 579 us
  other arithmetic  277 us (47%)
  local copies, waits for them, and re-layouts  250 us (43%)
  starting transfers between devices  35.8 us (6%)
  waiting for transfers between devices  15.4 us (3%)
    add x6, other arithmetic, advect(): center - 0.5 * east_wind * (eastern - western)  275 us
    slice x12, local copies, waits for them, and re-layouts, advect(): eastern = jnp.roll(center, -1, lat_dim + 1)  201 us
    unnamed x32, local copies, waits for them, and re-layouts  28.2 us
    slice x6, local copies, waits for them, and re-layouts, extended(): last = lax.slice_in_dim(shard, length - width, length, axis=dim)  18.3 us
    ppermute x6, starting transfers between devices, extended(): after = lax.ppermute(first, axis, down)  18.1 us
    ppermute x6, starting transfers between devices, extended(): before = lax.ppermute(last, axis, up)  17.7 us
    ppermute x6, waiting for transfers between devices, extended(): after = lax.ppermute(first, axis, down)  15.4 us
  transfers between devices with their start and end apart: 12, of which 4 were waited for; matrix products, arithmetic and copies ran while one was open for 22% of the time, Pallas kernels for 0%

commit v1 on v0

v1 whole, which is shorter than its diff:
```python
import functools

import jax
import jax.numpy as jnp
from jax import lax
from jax.experimental import pallas as pl
from jax.experimental.pallas import tpu as pltpu
from jax.sharding import PartitionSpec as P

NLON = 128
STEPS = 3
UNIT = STEPS * NLON
ROWS = 32
VMEM = 48 * 1024 * 1024


def stencil(c, east, west, north, south, coef):
    return coef[0] * c + coef[1] * east + coef[2] * west + coef[3] * north + coef[4] * south


def column_kernel(parts, sides, *refs):
    ins, tables, out = refs[: len(parts)], refs[len(parts)], refs[-1]
    for side, (names, first, count) in enumerate(sides):

        def source(line):
            part, at = divmod(line, STEPS)
            return ins[names[part]][at * NLON : (at + 1) * NLON, :]

        lines = count + 2 * STEPS
        got = {}
        for line in range(lines):
            got[0, line] = source(line)
            for step in range(1, STEPS + 1):
                mid = line - step
                if mid < step:
                    continue
                c = got[step - 1, mid]
                row = first + mid - 1
                value = stencil(
                    c,
                    pltpu.roll(c, NLON - 1, 0),
                    pltpu.roll(c, 1, 0),
                    got[step - 1, mid + 1],
                    got[step - 1, mid - 1],
                    [tables[k, row] for k in range(5)],
                )
                got.pop((step - 1, mid - 1))
                if step < STEPS:
                    got[step, mid] = value
                else:
                    at = sum(s[2] for s in sides[:side]) + mid - STEPS
                    out[at * NLON : (at + 1) * NLON, :] = value


def column_sweep(arrays, sides, width, coefs):
    total = sum(count for _, _, count in sides) * NLON
    in_specs = [
        pl.BlockSpec((UNIT, NLON), functools.partial(lambda i, r, c: (r, i + c), r=r, c=c)) for _, r, c in arrays
    ]
    in_specs.append(pl.BlockSpec(coefs.shape, lambda i: (0, 0, 0, 0)))
    work = total * width
    return pl.pallas_call(
        functools.partial(column_kernel, arrays, sides),
        grid=(width // NLON,),
        in_specs=in_specs,
        out_specs=pl.BlockSpec((total, NLON), lambda i: (0, i)),
        out_shape=jax.ShapeDtypeStruct((total, width), jnp.float32),
        compiler_params=pltpu.CompilerParams(vmem_limit_bytes=VMEM),
        cost_estimate=pl.CostEstimate(flops=work * 40, bytes_accessed=work * 12, transcendentals=0),
    )(*[a for a, _, _ in arrays], coefs)


def row_kernel(count, first, *refs):
    ins, coefs, out = refs[: count + 2], refs[count + 2], refs[-1]
    lines = (count + 2) * STEPS

    def group(g, carry):
        rows = pl.ds(pl.multiple_of(g * ROWS, ROWS), ROWS)
        got = {}
        for line in range(lines):
            part, at = divmod(line, STEPS)
            got[0, line] = ins[part][rows, at * NLON : (at + 1) * NLON]
            for step in range(1, STEPS + 1):
                mid = line - step
                if mid < step:
                    continue
                c = got[step - 1, mid]
                at = first + mid - 1
                value = stencil(
                    c.reshape(ROWS // 8, 8, NLON),
                    pltpu.roll(c, NLON - 1, 1).reshape(ROWS // 8, 8, NLON),
                    pltpu.roll(c, 1, 1).reshape(ROWS // 8, 8, NLON),
                    got[step - 1, mid + 1].reshape(ROWS // 8, 8, NLON),
                    got[step - 1, mid - 1].reshape(ROWS // 8, 8, NLON),
                    [coefs[k, at][None] for k in range(5)],
                ).reshape(ROWS, NLON)
                got.pop((step - 1, mid - 1))
                if step < STEPS:
                    got[step, mid] = value
                else:
                    to = mid - STEPS
                    out[rows, to * NLON : (to + 1) * NLON] = value
        return carry

    lax.fori_loop(0, out.shape[0] // ROWS, group, 0)


def row_sweep(arrays, first, coefs, out_rows, row_block, out_cols, col_block, buffer):
    block = NLON
    count = len(arrays) - 2
    rows = arrays[0][0].shape[0]
    in_specs = [pl.BlockSpec((block, UNIT), functools.partial(lambda i, c: (i, c), c=c)) for _, c in arrays]
    in_specs.append(pl.BlockSpec(coefs.shape, lambda i: (0, 0, 0, 0)))
    operands = [a for a, _ in arrays] + [coefs]
    aliases = {}
    if buffer is not None:
        in_specs.append(pl.BlockSpec(memory_space=pl.ANY))
        operands.append(buffer)
        aliases = {len(operands) - 1: 0}
    work = rows * count * UNIT
    return pl.pallas_call(
        functools.partial(row_kernel, count, first),
        grid=(rows // block,),
        in_specs=in_specs,
        out_specs=pl.BlockSpec((block, count * UNIT), lambda i: (row_block(i), col_block)),
        out_shape=jax.ShapeDtypeStruct((out_rows, out_cols), jnp.float32),
        input_output_aliases=aliases,
        compiler_params=pltpu.CompilerParams(vmem_limit_bytes=VMEM),
        cost_estimate=pl.CostEstimate(flops=work * 40, bytes_accessed=work * 12, transcendentals=0),
    )(*operands)


def exchange(first, last, axis):
    devices = lax.axis_size(axis)
    up = [(i, i + 1) for i in range(devices - 1)]
    down = [(j, i) for i, j in up]
    return lax.ppermute(last, axis, up), lax.ppermute(first, axis, down)


def coefficients(tables, offset, lines):
    east_wind, north_wind, diffuse_lon, diffuse_lat = tables
    made = jnp.stack(
        [
            1.0 - 2.0 * diffuse_lon - 2.0 * diffuse_lat,
            diffuse_lon - 0.5 * east_wind,
            diffuse_lon + 0.5 * east_wind,
            diffuse_lat - 0.5 * north_wind,
            diffuse_lat + 0.5 * north_wind,
        ]
    )
    edge = STEPS - 1
    made = jnp.pad(made, ((0, 0), (edge, edge), (0, 0)))
    return lax.dynamic_slice_in_dim(made, offset, lines + 2 * edge, 1)


def body(covariance, east_wind, north_wind, diffuse_lon, diffuse_lat):
    tables = (east_wind, north_wind, diffuse_lon, diffuse_lat)
    rows, cols = covariance.shape
    row_lines, col_lines = rows // NLON, cols // NLON
    row_units, col_units = rows // UNIT, cols // UNIT
    tiles = UNIT // NLON
    row_coefs = coefficients(tables, lax.axis_index("row") * row_lines, row_lines)
    row_coefs = jnp.broadcast_to(row_coefs[:, :, :, None], row_coefs.shape + (NLON,))
    col_coefs = coefficients(tables, lax.axis_index("col") * col_lines, col_lines)
    col_coefs = jnp.broadcast_to(col_coefs[:, :, None, :], col_coefs.shape[:2] + (8, NLON))

    if col_units == 1:
        pieces = [[0]]
    else:
        pieces = [[0, col_units - 1]]
        half = col_units // 2
        if col_units % 2 == 0 and col_units >= 6:
            pieces += [list(range(1, half + 1)), list(range(half + 1, col_units - 1))]
        elif col_units > 2:
            pieces += [list(range(1, col_units - 1))]

    def columns(units, low, high):
        parts = []
        for u in units:
            if parts and parts[-1][1] == u:
                parts[-1][1] = u + 1
            else:
                parts.append([u, u + 1])
        return jnp.concatenate([covariance[low:high, a * UNIT : b * UNIT] for a, b in parts], axis=1)

    halos = [exchange(columns(p, 0, UNIT), columns(p, rows - UNIT, rows), "row") for p in pieces]

    inner = None
    if row_units > 2:
        inner = column_sweep(
            [(covariance, r, 0) for r in range(row_units)],
            [(list(range(row_units)), STEPS, row_lines - 2 * STEPS)],
            cols,
            row_coefs,
        )

    outer = []
    where = {}
    for k, (units, (before, after)) in enumerate(zip(pieces, halos)):
        width = len(units) * UNIT
        if k == 0 and col_units > 1:
            own = columns(units, 0, rows)
            blocks = [(own, r, 0) for r in range(row_units)]
        else:
            blocks = [(covariance, r, units[0] * tiles) for r in range(row_units)]
        if row_units == 1:
            arrays = [(before, 0, 0), blocks[0], (after, 0, 0)]
            sides = [([0, 1, 2], 0, STEPS)]
        else:
            arrays = [(before, 0, 0), blocks[0], blocks[1], blocks[-2], blocks[-1], (after, 0, 0)]
            sides = [([0, 1, 2], 0, STEPS), ([3, 4, 5], row_lines - STEPS, STEPS)]
        outer.append(column_sweep(arrays, sides, width, row_coefs))
        for at, u in enumerate(units):
            where[u] = (k, at)

    out_blocks = rows // NLON
    halves = [list(range(col_units))]
    if len(pieces) == 3:
        halves = [list(range(half)), list(range(half, col_units))]

    edges = outer[0]
    outer_halo = exchange(edges[:, :UNIT], edges[:, -UNIT:], "col")
    out = None
    if inner is not None:
        inner_halo = exchange(inner[:, :UNIT], inner[:, cols - UNIT :], "col")
        arrays = [(inner_halo[0], 0)] + [(inner, u) for u in range(col_units)] + [(inner_halo[1], 0)]
        out = row_sweep(arrays, 0, col_coefs, rows, lambda i: i + tiles, cols, 0, out)

    def outer_row(i):
        return jnp.where(i < tiles, i, i + out_blocks - 2 * tiles) if row_units > 1 else i

    for h, units in enumerate(halves):
        arrays = []
        for u in [units[0] - 1] + units + [units[-1] + 1]:
            if u < 0:
                arrays.append((outer_halo[0], 0))
            elif u == col_units:
                arrays.append((outer_halo[1], 0))
            else:
                arrays.append((outer[where[u][0]], where[u][1]))
        out = row_sweep(arrays, units[0] * STEPS, col_coefs, rows, outer_row, cols, h, out)
    return out


def solution(mesh):
    return jax.shard_map(
        body,
        mesh=mesh,
        in_specs=(P("row", "col"), P(), P(), P(), P()),
        out_specs=P("row", "col"),
        check_vma=False,
    )
```

time: 588 us -> 201 us (0.34)
  the two profiles are of different devices: /device:TPU:10 before, /device:TPU:27 now
where the time goes in v1:
time: 201 us; the launch traced here: 199 us
  Pallas kernels  136 us (68%)
  starting transfers between devices  27.6 us (14%)
  local copies, waits for them, and re-layouts  20.4 us (10%)
  waiting for transfers between devices  10 us (5%)
  other arithmetic  4.82 us (2%)
    pallas_call x3, Pallas kernels, row_sweep(): pl.pallas_call(functools.partial(row_kernel, count, first), grid=(rows //...  71.2 us
    pallas_call x4, Pallas kernels, column_sweep(): pl.pallas_call(functools.partial(column_kernel, arrays, sides), grid=(wid...  65 us
    ppermute x10, starting transfers between devices, exchange(): return (lax.ppermute(last, axis, up), lax.ppermute(first, axis, down))  27.6 us
    slice x4, local copies, waits for them, and re-layouts, columns(): covariance[low:high, a * UNIT:b * UNIT]  12.5 us
    ppermute x10, waiting for transfers between devices, exchange(): return (lax.ppermute(last, axis, up), lax.ppermute(first, axis, down))  10 us
    concatenate x3, other arithmetic, columns(): jnp.concatenate([covariance[low:high, a * UNIT:b * UNIT] for a, b in part...  4.78 us
  transfers between devices with their start and end apart: 10, of which 2 were waited for; matrix products, arithmetic and copies ran while one was open for 11% of the time, Pallas kernels for 59%

profile of v1, /device:TPU:27, one launch (start us, length us, event | category | flops | bytes accessed | tf_op | source)
XLA Modules:
  0.0 199.3 jit_solution(5505269494685037954)
XLA Ops:
  0.0 1.8 fusion
  1.8 1.1 pad_maximum_fusion.1
  2.9 3.7 %collective-permute-start.4 = (f32[384,768]{1,0:T(8,128)}, f32[384,768]{1,0:T(8,128)S(1)}, u32[]{:S(2)}, u32[]{:S(2)}) collective-permute-start(f32[384,768]{1,0:T(8,128)} %pad_maximum_fusion.1), channel_id=1, source_target_pairs={{0,4},{4,8},{8,12},{12,16},{16,20},{20,24},{24,28},{1,5},{5,9},{9,... | collective-permute-start | bytes 3538952 | tf_op jit(solution)/shard_map/ppermute | solution.py:137
  6.5 1.1 pad_maximum_fusion.2
  7.7 1.9 collective-permute-start.5
  9.6 3.2 %fusion.2 = (f32[384,768]{1,0:T(8,128)}, f32[384,768]{1,0:T(8,128)}) fusion(f32[1536,3072]{1,0:T(8,128)} %refs_3_.5), kind=kLoop, calls=%fused_computation.12 | loop fusion | bytes 4718592 | tf_op jit(solution)/shard_map/slice | solution.py:184
  12.8 2.5 %collective-permute-start.3 = (f32[384,768]{1,0:T(8,128)}, f32[384,768]{1,0:T(8,128)}, u32[]{:S(2)}, u32[]{:S(2)}) collective-permute-start(f32[384,768]{1,0:T(8,128)} %get-tuple-element.11), channel_id=1, source_target_pairs={{4,0},{8,4},{12,8},{16,12},{20,16},{24,20},{28,24},{5,1},{9,5},{13... | collective-permute-start | bytes 3538952 | tf_op jit(solution)/shard_map/ppermute | solution.py:137
  15.4 0.0 copy-start.7
  15.4 0.0 copy-start.8
  15.4 0.0 copy-start.9
  15.4 0.0 copy-start.10
  15.4 4.0 %collective-permute-start.2 = (f32[384,768]{1,0:T(8,128)}, f32[384,768]{1,0:T(8,128)}, u32[]{:S(2)}, u32[]{:S(2)}) collective-permute-start(f32[384,768]{1,0:T(8,128)} %get-tuple-element.12), channel_id=1, source_target_pairs={{0,4},{4,8},{8,12},{12,16},{16,20},{20,24},{24,28},{1,5},{5,9},{9,... | collective-permute-start | bytes 3538952 | tf_op jit(solution)/shard_map/ppermute | solution.py:137
  19.5 4.8 %fusion.3 = (f32[384,1536]{1,0:T(8,128)}, f32[384,1536]{1,0:T(8,128)}) fusion(f32[1536,3072]{1,0:T(8,128)} %refs_3_.5), kind=kLoop, calls=%fused_computation.13 | loop fusion | bytes 9437184 | tf_op jit(solution)/shard_map/slice | solution.py:184
  24.3 1.9 collective-permute-start.1
  26.3 0.0 copy-done.10
  26.4 1.4 broadcast_in_dim.4.refs_6_.refs_4_
  27.8 27.7 %shard_map.58.refs_1_.refs_2_.refs_3_.refs_4_.refs_5_.refs_6_.refs_7_.refs_8_ = f32[768,3072]{1,0:T(8,128)} custom-call(f32[1536,3072]{1,0:T(8,128)} %refs_3_.5, f32[1536,3072]{1,0:T(8,128)} %refs_3_.5, f32[1536,3072]{1,0:T(8,128)} %refs_3_.5, f32[1536,3072]{1,0:T(8,128)} %refs_3_.5, f32[5,16,128,128]{3,2,1,0:T(8,128)S(1)} %broadcast_in_dim.4.refs_6_.refs_4_), custom_call_target="tpu_custom_call" | custom-call | flops 94371840 | bytes 28311552 | tf_op jit(solution)/shard_map/pallas_call | solution.py:62
  55.5 0.0 copy-done
  55.5 2.8 %fusion.4 = (f32[768,384]{1,0:T(8,128)S(1)}, f32[768,384]{1,0:T(8,128)}) fusion(f32[768,3072]{1,0:T(8,128)} %shard_map.58.refs_1_.refs_2_.refs_3_.refs_4_.refs_5_.refs_6_.refs_7_.refs_8_), kind=kLoop, calls=%fused_computation.14 | loop fusion | bytes 4718592 | tf_op jit(solution)/shard_map/slice | solution.py:225
  58.3 0.0 collective-permute-done.4.refs_0_
  58.3 4.5 %collective-permute-start = (f32[384,1536]{1,0:T(8,128)}, f32[384,1536]{1,0:T(8,128)}, u32[]{:S(2)}, u32[]{:S(2)}) collective-permute-start(f32[384,1536]{1,0:T(8,128)} %get-tuple-element.14), channel_id=1, source_target_pairs={{0,4},{4,8},{8,12},{12,16},{16,20},{20,24},{24,28},{1,5},{5,9},{9,... | collective-permute-start | bytes 7077896 | tf_op jit(solution)/shard_map/ppermute | solution.py:137
  62.9 0.0 collective-permute-done.5.refs_5_
  62.9 2.1 %collective-permute-start.9 = (f32[768,384]{1,0:T(8,128)S(1)}, f32[768,384]{1,0:T(8,128)S(1)}, u32[]{:S(2)}, u32[]{:S(2)}) collective-permute-start(f32[768,384]{1,0:T(8,128)S(1)} %get-tuple-element.15), channel_id=1, source_target_pairs={{1,0},{2,1},{3,2},{5,4},{6,5},{7,6},{9,8},{10,9},{11,10},{13,12},{... | collective-permute-start | bytes 3538952 | tf_op jit(solution)/shard_map/ppermute | solution.py:137
  65.1 2.7 %fusion.1 = (f32[1536,384]{1,0:T(8,128)S(1)}, f32[1536,384]{1,0:T(8,128)S(1)}) fusion(f32[1536,3072]{1,0:T(8,128)} %refs_3_.5), kind=kLoop, calls=%fused_computation.11 | loop fusion | bytes 9437184 | tf_op jit(solution)/shard_map/slice | solution.py:184
  67.8 0.0 copy-done.2
  67.8 0.0 copy-start.3
  67.8 2.6 %pad_maximum_fusion.refs_1_.refs_2_.refs_3_.refs_4_ = f32[1536,768]{1,0:T(8,128)} fusion(f32[1536,384]{1,0:T(8,128)S(1)} %get-tuple-element.10, f32[1536,384]{1,0:T(8,128)S(1)} %get-tuple-element.9), kind=kLoop, calls=%fused_computation | loop fusion | flops 1179648 | bytes 9437184 | tf_op jit(solution)/shard_map/concatenate | solution.py:184
  70.3 9.3 %shard_map.57.refs_1_.refs_4_ = f32[768,768]{1,0:T(8,128)S(1)} custom-call(f32[384,768]{1,0:T(8,128)S(1)} %collective-permute-done.4.refs_0_, f32[1536,768]{1,0:T(8,128)} %pad_maximum_fusion.refs_1_.refs_2_.refs_3_.refs_4_, f32[1536,768]{1,0:T(8,128)} %pad_maximum_fusion.refs_1_.refs_2_.refs_3_.refs_4_, ...), custom_call_target="tpu_custom_call" | custom-call | flops 23592960 | bytes 7077888 | tf_op jit(solution)/shard_map/pallas_call | solution.py:62
  79.7 0.0 collective-permute-done.3.refs_5_
  79.7 1.3 collective-permute-start.8
  81.0 1.5 fusion.5
  82.5 0.0 collective-permute-done.2.refs_0_
  82.5 1.3 collective-permute-start.7
  83.8 5.3 %collective-permute-done.9.refs_9_ = f32[768,384]{1,0:T(8,128)S(1)} collective-permute-done((f32[768,384]{1,0:T(8,128)S(1)}, f32[768,384]{1,0:T(8,128)S(1)}, u32[]{:S(2)}, u32[]{:S(2)}) %collective-permute-start.9) | collective-permute-done | bytes 1179680 | tf_op jit(solution)/shard_map/ppermute | solution.py:137
  89.1 1.0 copy-done.4
  90.1 4.3 %collective-permute-start.6 = (f32[768,384]{1,0:T(8,128)}, f32[768,384]{1,0:T(8,128)S(1)}, u32[]{:S(2)}, u32[]{:S(2)}) collective-permute-start(f32[768,384]{1,0:T(8,128)} %get-tuple-element.18), channel_id=1, source_target_pairs={{1,0},{2,1},{3,2},{5,4},{6,5},{7,6},{9,8},{10,9},{11,10},{13,12},{... | collective-permute-start | bytes 3538952 | tf_op jit(solution)/shard_map/ppermute | solution.py:137
  94.4 0.9 pad_dynamic-slice_fusion
  95.3 0.0 copy-start.5
  95.3 9.9 %shard_map.56.refs_2_.refs_3_ = f32[768,768]{1,0:T(8,128)S(1)} custom-call(f32[384,768]{1,0:T(8,128)} %collective-permute-done.2.refs_0_, f32[1536,3072]{1,0:T(8,128)} %refs_3_.5, f32[1536,3072]{1,0:T(8,128)} %refs_3_.5, f32[1536,3072]{1,0:T(8,128)} %refs_3_.5, f32[1536,3072]{1,0:T(8,128)} %refs_3_.5, f32[384,768]{1,0:T(8,128)} %collective-permute-done.3.refs_5_, ...), custom_call_target="tpu_custom_call" | custom-call | flops 23592960 | bytes 7077888 | tf_op jit(solution)/shard_map/pallas_call | solution.py:62
  105.2 4.7 %collective-permute-done.8.refs_0_ = f32[768,384]{1,0:T(8,128)} collective-permute-done((f32[768,384]{1,0:T(8,128)}, f32[768,384]{1,0:T(8,128)}, u32[]{:S(2)}, u32[]{:S(2)}) %collective-permute-start.8) | collective-permute-done | bytes 1179680 | tf_op jit(solution)/shard_map/ppermute | solution.py:137
  110.0 34.3 %shard_map.59.refs_7_ = f32[1536,3072]{1,0:T(8,128)} custom-call(f32[768,384]{1,0:T(8,128)} %collective-permute-done.8.refs_0_, f32[768,3072]{1,0:T(8,128)} %shard_map.58.refs_1_.refs_2_.refs_3_.refs_4_.refs_5_.refs_6_.refs_7_.refs_8_, f32[768,3072]{1,0:T(8,128)} %shard_map.58.refs_1_.refs_2_.refs_3_.refs_4_.refs_5_.refs_6_.refs_7_.refs_8_, ...), custom_call_target="tpu_custom_call" | custom-call | flops 94371840 | bytes 28311552 | tf_op jit(solution)/shard_map/pallas_call | solution.py:121
  144.3 0.0 collective-permute-done.1.refs_5_
  144.3 0.0 collective-permute-done.refs_0_
  144.3 18.1 %shard_map.55.refs_2_.refs_3_.refs_4_.refs_5_.refs_0_.refs_1_ = f32[768,1536]{1,0:T(8,128)} custom-call(f32[384,1536]{1,0:T(8,128)} %collective-permute-done.refs_0_, f32[1536,3072]{1,0:T(8,128)} %refs_3_.5, f32[1536,3072]{1,0:T(8,128)} %refs_3_.5, f32[1536,3072]{1,0:T(8,128)} %refs_3_.5, f32[1536,3072]{1,0:T(8,128)} %refs_3_.5, ...), custom_call_target="tpu_custom_call" | custom-call | flops 47185920 | bytes 14155776 | tf_op jit(solution)/shard_map/pallas_call | solution.py:62
  162.4 0.0 collective-permute-done.7.refs_0_
  162.4 18.5 %shard_map.60.refs_7_ = f32[1536,3072]{1,0:T(8,128)} custom-call(f32[768,384]{1,0:T(8,128)} %collective-permute-done.7.refs_0_, f32[768,768]{1,0:T(8,128)S(1)} %shard_map.57.refs_1_.refs_4_, f32[768,1536]{1,0:T(8,128)} %shard_map.55.refs_2_.refs_3_.refs_4_.refs_5_.refs_0_.refs_1_, ...), custom_call_target="tpu_custom_call", output_to_operand_aliasing={{}: (7, {})} | custom-call | flops 47185920 | bytes 14155776 | tf_op jit(solution)/shard_map/pallas_call | solution.py:121
  180.9 0.0 collective-permute-done.6.refs_5_
  180.9 18.4 %shard_map.61 = f32[1536,3072]{1,0:T(8,128)} custom-call(f32[768,1536]{1,0:T(8,128)} %shard_map.55.refs_2_.refs_3_.refs_4_.refs_5_.refs_0_.refs_1_, f32[768,1536]{1,0:T(8,128)} %shard_map.55.refs_2_.refs_3_.refs_4_.refs_5_.refs_0_.refs_1_, f32[768,768]{1,0:T(8,128)S(1)} %shard_map.56.refs_2_.refs_3_, ...), custom_call_target="tpu_custom_call", output_to_operand_aliasing={{}: (7, {})} | custom-call | flops 47185920 | bytes 14155776 | tf_op jit(solution)/shard_map/pallas_call | solution.py:121
  (19 shorter events, 0.1 us)
Async XLA Ops:
  2.9 55.5 %collective-permute-start.4 = (f32[384,768]{1,0:T(8,128)}, f32[384,768]{1,0:T(8,128)S(1)}, u32[]{:S(2)}, u32[]{:S(2)}) collective-permute-start(f32[384,768]{1,0:T(8,128)} %pad_maximum_fusion.1), channel_id=1, source_target_pairs={{0,4},{4,8},{8,12},{12,16},{16,20},{20,24},{24,28},{1,5},{5,9},{9,... | collective-permute-start | bytes 3538952 | tf_op jit(solution)/shard_map/ppermute | solution.py:137
  7.7 55.2 %collective-permute-start.5 = (f32[384,768]{1,0:T(8,128)}, f32[384,768]{1,0:T(8,128)S(1)}, u32[]{:S(2)}, u32[]{:S(2)}) collective-permute-start(f32[384,768]{1,0:T(8,128)} %pad_maximum_fusion.2), channel_id=1, source_target_pairs={{4,0},{8,4},{12,8},{16,12},{20,16},{24,20},{28,24},{5,1},{9,5},{13... | collective-permute-start | bytes 3538952 | tf_op jit(solution)/shard_map/ppermute | solution.py:137
  12.8 66.9 %collective-permute-start.3 = (f32[384,768]{1,0:T(8,128)}, f32[384,768]{1,0:T(8,128)}, u32[]{:S(2)}, u32[]{:S(2)}) collective-permute-start(f32[384,768]{1,0:T(8,128)} %get-tuple-element.11), channel_id=1, source_target_pairs={{4,0},{8,4},{12,8},{16,12},{20,16},{24,20},{28,24},{5,1},{9,5},{13... | collective-permute-start | bytes 3538952 | tf_op jit(solution)/shard_map/ppermute | solution.py:137
  15.4 10.9 %copy-start.7 = (f32[96,128]{1,0:T(8,128)S(1)}, f32[96,128]{1,0:T(8,128)}, u32[]{:S(2)}) copy-start(f32[96,128]{1,0:T(8,128)} %param.8) | copy-start | bytes 147460
  15.4 10.9 %copy-start.8 = (f32[96,128]{1,0:T(8,128)S(1)}, f32[96,128]{1,0:T(8,128)}, u32[]{:S(2)}) copy-start(f32[96,128]{1,0:T(8,128)} %param.9) | copy-start | bytes 147460
  15.4 10.9 %copy-start.9 = (f32[96,128]{1,0:T(8,128)S(1)}, f32[96,128]{1,0:T(8,128)}, u32[]{:S(2)}) copy-start(f32[96,128]{1,0:T(8,128)} %param.6) | copy-start | bytes 147460
  15.4 10.9 %copy-start.10 = (f32[96,128]{1,0:T(8,128)S(1)}, f32[96,128]{1,0:T(8,128)}, u32[]{:S(2)}) copy-start(f32[96,128]{1,0:T(8,128)} %param.7) | copy-start | bytes 147460
  15.4 67.1 %collective-permute-start.2 = (f32[384,768]{1,0:T(8,128)}, f32[384,768]{1,0:T(8,128)}, u32[]{:S(2)}, u32[]{:S(2)}) collective-permute-start(f32[384,768]{1,0:T(8,128)} %get-tuple-element.12), channel_id=1, source_target_pairs={{0,4},{4,8},{8,12},{12,16},{16,20},{20,24},{24,28},{1,5},{5,9},{9,... | collective-permute-start | bytes 3538952 | tf_op jit(solution)/shard_map/ppermute | solution.py:137
  24.3 120.0 %collective-permute-start.1 = (f32[384,1536]{1,0:T(8,128)}, f32[384,1536]{1,0:T(8,128)}, u32[]{:S(2)}, u32[]{:S(2)}) collective-permute-start(f32[384,1536]{1,0:T(8,128)} %get-tuple-element.13), channel_id=1, source_target_pairs={{4,0},{8,4},{12,8},{16,12},{20,16},{24,20},{28,24},{5,1},{9,5},{13... | collective-permute-start | bytes 7077896 | tf_op jit(solution)/shard_map/ppermute | solution.py:137
  26.4 1.5 copy-start.6
  27.8 27.7 %copy-start = (f32[5,16,128,128]{3,2,1,0:T(8,128)}, f32[5,16,128,128]{3,2,1,0:T(8,128)S(1)}, u32[]{:S(2)}) copy-start(f32[5,16,128,128]{3,2,1,0:T(8,128)S(1)} %broadcast_in_dim.4.refs_6_.refs_4_) | copy-start | bytes 15728644
  58.3 85.9 %collective-permute-start = (f32[384,1536]{1,0:T(8,128)}, f32[384,1536]{1,0:T(8,128)}, u32[]{:S(2)}, u32[]{:S(2)}) collective-permute-start(f32[384,1536]{1,0:T(8,128)} %get-tuple-element.14), channel_id=1, source_target_pairs={{0,4},{4,8},{8,12},{12,16},{16,20},{20,24},{24,28},{1,5},{5,9},{9,... | collective-permute-start | bytes 7077896 | tf_op jit(solution)/shard_map/ppermute | solution.py:137
  62.9 4.9 %copy-start.2 = (f32[384,768]{1,0:T(8,128)}, f32[384,768]{1,0:T(8,128)S(1)}, u32[]{:S(2)}) copy-start(f32[384,768]{1,0:T(8,128)S(1)} %collective-permute-done.5.refs_5_) | copy-start | bytes 3538948
  62.9 26.2 %collective-permute-start.9 = (f32[768,384]{1,0:T(8,128)S(1)}, f32[768,384]{1,0:T(8,128)S(1)}, u32[]{:S(2)}, u32[]{:S(2)}) collective-permute-start(f32[768,384]{1,0:T(8,128)S(1)} %get-tuple-element.15), channel_id=1, source_target_pairs={{1,0},{2,1},{3,2},{5,4},{6,5},{7,6},{9,8},{10,9},{11,10},{13,12},{... | collective-permute-start | bytes 3538952 | tf_op jit(solution)/shard_map/ppermute | solution.py:137
  67.8 2.6 %copy-start.3 = (f32[384,768]{1,0:T(8,128)S(1)}, f32[384,768]{1,0:T(8,128)}, u32[]{:S(2)}) copy-start(f32[384,768]{1,0:T(8,128)} %copy-done.2) | copy-start | bytes 3538948
  79.7 82.8 %copy-start.1 = (f32[768,768]{1,0:T(8,128)}, f32[768,768]{1,0:T(8,128)S(1)}, u32[]{:S(2)}) copy-start(f32[768,768]{1,0:T(8,128)S(1)} %shard_map.57.refs_1_.refs_4_) | copy-start | bytes 7077892
  79.7 30.2 %collective-permute-start.8 = (f32[768,384]{1,0:T(8,128)}, f32[768,384]{1,0:T(8,128)}, u32[]{:S(2)}, u32[]{:S(2)}) collective-permute-start(f32[768,384]{1,0:T(8,128)} %get-tuple-element.16), channel_id=1, source_target_pairs={{0,1},{1,2},{2,3},{4,5},{5,6},{6,7},{8,9},{9,10},{10,11},{12,13},{... | collective-permute-start | bytes 3538952 | tf_op jit(solution)/shard_map/ppermute | solution.py:137
  82.5 79.9 %collective-permute-start.7 = (f32[768,384]{1,0:T(8,128)}, f32[768,384]{1,0:T(8,128)}, u32[]{:S(2)}, u32[]{:S(2)}) collective-permute-start(f32[768,384]{1,0:T(8,128)} %get-tuple-element.17), channel_id=1, source_target_pairs={{0,1},{1,2},{2,3},{4,5},{5,6},{6,7},{8,9},{9,10},{10,11},{12,13},{... | collective-permute-start | bytes 3538952 | tf_op jit(solution)/shard_map/ppermute | solution.py:137
  89.1 1.0 copy-start.4
  90.1 90.8 %collective-permute-start.6 = (f32[768,384]{1,0:T(8,128)}, f32[768,384]{1,0:T(8,128)S(1)}, u32[]{:S(2)}, u32[]{:S(2)}) collective-permute-start(f32[768,384]{1,0:T(8,128)} %get-tuple-element.18), channel_id=1, source_target_pairs={{1,0},{2,1},{3,2},{5,4},{6,5},{7,6},{9,8},{10,9},{11,10},{13,12},{... | collective-permute-start | bytes 3538952 | tf_op jit(solution)/shard_map/ppermute | solution.py:137
  95.3 14.7 %copy-start.5 = (f32[768,384]{1,0:T(8,128)S(1)}, f32[768,384]{1,0:T(8,128)}, u32[]{:S(2)}) copy-start(f32[768,384]{1,0:T(8,128)} %copy-done.4) | copy-start | bytes 3538948

commit v2 on v1

v2 whole, which is shorter than its diff:
```python
import functools

import jax
import jax.numpy as jnp
from jax import lax
from jax.experimental import pallas as pl
from jax.experimental.pallas import tpu as pltpu
from jax.sharding import PartitionSpec as P

NLON = 128
STEPS = 3
UNIT = STEPS * NLON
WIDE = 256
BLOCK = 192
VMEM = 52 * 1024 * 1024


OFFSETS = [(y, x) for y in range(-STEPS, STEPS + 1) for x in range(-STEPS + abs(y), STEPS + 1 - abs(y))]


def power_kernel(east_wind, north_wind, diffuse_lon, diffuse_lat, plain, rolled):
    lon, lat = diffuse_lon[...], diffuse_lat[...]
    half_east, half_north = 0.5 * east_wind[...], 0.5 * north_wind[...]
    one = {
        (0, 0): 1.0 - 2.0 * lon - 2.0 * lat,
        (0, 1): lon - half_east,
        (0, -1): lon + half_east,
        (1, 0): lat - half_north,
        (-1, 0): lat + half_north,
    }
    lines = lon.shape[0]
    line = lax.broadcasted_iota(jnp.int32, lon.shape, 0)

    def seen(field, y, x):
        if x:
            return pltpu.roll(field, -x % NLON, 1)
        if y:
            edge = lines - 1 if y > 0 else 0
            return jnp.where(line == edge, 0.0, pltpu.roll(field, -y % lines, 0))
        return field

    power = dict(one)
    for _ in range(STEPS - 1):
        made = {}
        for (y, x), field in power.items():
            for (sy, sx), scale in one.items():
                term = scale * seen(field, sy, sx)
                at = (y + sy, x + sx)
                made[at] = made[at] + term if at in made else term
        power = made
    for k, (y, x) in enumerate(OFFSETS):
        plain[k] = power[y, x]
        rolled[k] = pltpu.roll(power[y, x], x % NLON, 1)


def powers(tables):
    shape = jax.ShapeDtypeStruct((len(OFFSETS),) + tables[0].shape, jnp.float32)
    return pl.pallas_call(
        power_kernel,
        out_shape=(shape, shape),
        compiler_params=pltpu.CompilerParams(vmem_limit_bytes=VMEM),
        cost_estimate=pl.CostEstimate(flops=10**7, bytes_accessed=10**7, transcendentals=0),
    )(*tables)


def split(value):
    high = value.astype(jnp.bfloat16)
    return high, (value - high.astype(jnp.float32)).astype(jnp.bfloat16)


def block_kernel(made, transposed, offset, table, out):
    base = offset[0] + pl.program_id(0) * made
    sub = lax.broadcasted_iota(jnp.int32, (NLON, NLON), 0)
    lane = lax.broadcasted_iota(jnp.int32, (NLON, NLON), 1)
    away = (sub - lane if transposed else lane - sub) & (NLON - 1)
    read = made + 2 * STEPS
    for a in range(made):
        for b in range(read):
            y = b - a - STEPS
            value = jnp.zeros((NLON, NLON), jnp.float32)
            for k, (oy, x) in enumerate(OFFSETS):
                if oy == y:
                    line = table[k, pl.ds(base + a, 1), :]
                    value = jnp.where(away == x % NLON, jnp.broadcast_to(line, (NLON, NLON)), value)
            high, low = split(value)
            mine, theirs = slice(a * NLON, (a + 1) * NLON), slice(b * NLON, (b + 1) * NLON)
            if transposed:
                out[0, theirs, mine] = high
                out[0, slice((read + b) * NLON, (read + b + 1) * NLON), mine] = low
            else:
                out[0, mine, theirs] = high
                out[0, slice((made + a) * NLON, (made + a + 1) * NLON), theirs] = low


def blocks_of(table, offset, groups, made, transposed):
    read = made + 2 * STEPS
    shape = (2 * read * NLON, made * NLON) if transposed else (2 * made * NLON, read * NLON)
    return pl.pallas_call(
        functools.partial(block_kernel, made, transposed),
        grid=(groups,),
        in_specs=[
            pl.BlockSpec(memory_space=pltpu.SMEM),
            pl.BlockSpec(table.shape, lambda i: (0, 0, 0)),
        ],
        out_specs=pl.BlockSpec((1,) + shape, lambda i: (i, 0, 0)),
        out_shape=jax.ShapeDtypeStruct((groups,) + shape, jnp.bfloat16),
        compiler_params=pltpu.CompilerParams(vmem_limit_bytes=VMEM),
        cost_estimate=pl.CostEstimate(flops=10**7, bytes_accessed=2 * 10**7, transcendentals=0),
    )(offset.reshape(1).astype(jnp.int32), table)


def dot(a, b):
    return jnp.dot(a, b, preferred_element_type=jnp.float32)


def column_kernel(sides, *refs):
    ins, tables, out, high, low = refs[:-4], refs[-4], refs[-3], refs[-2], refs[-1]
    for n, ref in enumerate(ins):
        rows = slice(n * UNIT, (n + 1) * UNIT)
        high[rows, :], low[rows, :] = split(ref[...])
    for at, (start, group) in enumerate(sides):
        rows = slice(start * UNIT, (start + 3) * UNIT)
        both = dot(tables[group], high[rows, :])
        other = dot(tables[group, :UNIT, :], low[rows, :])
        out[at * UNIT : (at + 1) * UNIT, :] = both[:UNIT] + (both[UNIT:] + other)


def column_sweep(arrays, sides, width, tables):
    total = len(sides) * UNIT
    tile = WIDE if all(n % WIDE == 0 for n in [width] + [c for _, _, c in arrays]) else UNIT
    in_specs = [
        pl.BlockSpec((UNIT, tile), functools.partial(lambda i, r, c: (r, i + c), r=r, c=c // tile))
        for _, r, c in arrays
    ]
    in_specs.append(pl.BlockSpec(tables.shape, lambda i: (0, 0, 0), pipeline_mode=pl.Buffered(1)))
    scratch = pltpu.VMEM((len(arrays) * UNIT, tile), jnp.bfloat16)
    work = total * width
    return pl.pallas_call(
        functools.partial(column_kernel, sides),
        grid=(width // tile,),
        in_specs=in_specs,
        out_specs=pl.BlockSpec((total, tile), lambda i: (0, i)),
        out_shape=jax.ShapeDtypeStruct((total, width), jnp.float32),
        scratch_shapes=[scratch, scratch],
        compiler_params=pltpu.CompilerParams(vmem_limit_bytes=VMEM),
        cost_estimate=pl.CostEstimate(flops=work * 2 * 1152 * 3, bytes_accessed=work * 12, transcendentals=0),
    )(*[a for a, _, _ in arrays], tables)


def row_kernel(count, *refs):
    ins, tables, out, both = refs[: count + 2], refs[count + 2], refs[-2], refs[-1]
    rows = out.shape[0]
    read = (2 + 2 * STEPS) * NLON
    for n, ref in enumerate(ins):
        cols = slice(n * UNIT, (n + 1) * UNIT)
        both[:rows, cols], both[rows:, cols] = split(ref[...])
    for pair in range(count * STEPS // 2):
        cols = slice(pair * 2 * NLON, pair * 2 * NLON + read)
        first = dot(both[:, cols], tables[pair, :read, :])
        other = dot(both[:rows, cols], tables[pair, read:, :])
        out[:, pair * 2 * NLON : (pair + 1) * 2 * NLON] = first[:rows] + (first[rows:] + other)


def row_sweep(arrays, part, tables, out_rows, row_block, out_cols, col_block, buffer):
    count = len(arrays) - 2
    rows = arrays[0][0].shape[0]
    pairs = count * STEPS // 2
    in_specs = [pl.BlockSpec((BLOCK, UNIT), functools.partial(lambda i, c: (i, c), c=c)) for _, c in arrays]
    in_specs.append(
        pl.BlockSpec((pairs,) + tables.shape[1:], lambda i: (part, 0, 0), pipeline_mode=pl.Buffered(1))
    )
    operands = [a for a, _ in arrays] + [tables]
    aliases = {}
    if buffer is not None:
        in_specs.append(pl.BlockSpec(memory_space=pl.ANY))
        operands.append(buffer)
        aliases = {len(operands) - 1: 0}
    work = rows * count * UNIT
    return pl.pallas_call(
        functools.partial(row_kernel, count),
        grid=(rows // BLOCK,),
        in_specs=in_specs,
        out_specs=pl.BlockSpec((BLOCK, count * UNIT), lambda i: (row_block(i), col_block)),
        out_shape=jax.ShapeDtypeStruct((out_rows, out_cols), jnp.float32),
        input_output_aliases=aliases,
        scratch_shapes=[pltpu.VMEM((2 * BLOCK, len(arrays) * UNIT), jnp.bfloat16)],
        compiler_params=pltpu.CompilerParams(vmem_limit_bytes=VMEM),
        cost_estimate=pl.CostEstimate(flops=work * 2 * 1024 * 3, bytes_accessed=work * 12, transcendentals=0),
    )(*operands)


def exchange(first, last, axis):
    devices = lax.axis_size(axis)
    up = [(i, i + 1) for i in range(devices - 1)]
    down = [(j, i) for i, j in up]
    return lax.ppermute(last, axis, up), lax.ppermute(first, axis, down)


def body(covariance, east_wind, north_wind, diffuse_lon, diffuse_lat):
    tables = (east_wind, north_wind, diffuse_lon, diffuse_lat)
    rows, cols = covariance.shape
    row_lines, col_lines = rows // NLON, cols // NLON
    row_units, col_units = rows // UNIT, cols // UNIT
    plain, rolled = powers(tables)
    row_tables = blocks_of(rolled, lax.axis_index("row") * row_lines, row_units, STEPS, False)
    col_tables = blocks_of(plain, lax.axis_index("col") * col_lines, col_lines // 2, 2, True)

    if col_units == 1:
        pieces = [[0]]
    else:
        pieces = [[0, col_units - 1]]
        half = col_units // 2
        if col_units % 2 == 0 and col_units >= 6:
            pieces += [list(range(1, half + 1)), list(range(half + 1, col_units - 1))]
        elif col_units > 2:
            pieces += [list(range(1, col_units - 1))]

    def columns(units, low, high):
        parts = []
        for u in units:
            if parts and parts[-1][1] == u:
                parts[-1][1] = u + 1
            else:
                parts.append([u, u + 1])
        return jnp.concatenate([covariance[low:high, a * UNIT : b * UNIT] for a, b in parts], axis=1)

    halos = [exchange(columns(p, 0, UNIT), columns(p, rows - UNIT, rows), "row") for p in pieces]

    inner = None
    if row_units > 2:
        inner = column_sweep(
            [(covariance, r, 0) for r in range(row_units)],
            [(u, u + 1) for u in range(row_units - 2)],
            cols,
            row_tables,
        )

    outer = []
    where = {}
    for k, (units, (before, after)) in enumerate(zip(pieces, halos)):
        width = len(units) * UNIT
        if k == 0 and col_units > 1:
            own = columns(units, 0, rows)
            blocks = [(own, r, 0) for r in range(row_units)]
        else:
            blocks = [(covariance, r, units[0] * UNIT) for r in range(row_units)]
        if row_units == 1:
            arrays = [(before, 0, 0), blocks[0], (after, 0, 0)]
            sides = [(0, 0)]
        else:
            arrays = [(before, 0, 0), blocks[0], blocks[1], blocks[-2], blocks[-1], (after, 0, 0)]
            sides = [(0, 0), (3, row_units - 1)]
        outer.append(column_sweep(arrays, sides, width, row_tables))
        for at, u in enumerate(units):
            where[u] = (k, at)

    out_blocks, tiles = rows // BLOCK, UNIT // BLOCK
    halves = [list(range(col_units))]
    if len(pieces) == 3:
        halves = [list(range(half)), list(range(half, col_units))]

    edges = outer[0]
    outer_halo = exchange(edges[:, :UNIT], edges[:, -UNIT:], "col")
    out = None
    if inner is not None:
        inner_halo = exchange(inner[:, :UNIT], inner[:, cols - UNIT :], "col")
        arrays = [(inner_halo[0], 0)] + [(inner, u) for u in range(col_units)] + [(inner_halo[1], 0)]
        out = row_sweep(arrays, 0, col_tables, rows, lambda i: i + tiles, cols, 0, out)

    def outer_row(i):
        return jnp.where(i < tiles, i, i + out_blocks - 2 * tiles) if row_units > 1 else i

    for h, units in enumerate(halves):
        arrays = []
        for u in [units[0] - 1] + units + [units[-1] + 1]:
            if u < 0:
                arrays.append((outer_halo[0], 0))
            elif u == col_units:
                arrays.append((outer_halo[1], 0))
            else:
                arrays.append((outer[where[u][0]], where[u][1]))
        out = row_sweep(arrays, h, col_tables, rows, outer_row, cols, h, out)
    return out


def solution(mesh):
    return jax.shard_map(
        body,
        mesh=mesh,
        in_specs=(P("row", "col"), P(), P(), P(), P()),
        out_specs=P("row", "col"),
        check_vma=False,
    )
```

time: 201 us -> 205 us (1.020)
  the two profiles are of different devices: /device:TPU:27 before, /device:TPU:6 now
where the time goes in v2:
time: 205 us
  Pallas kernels  128 us (62%)
  local copies, waits for them, and re-layouts  25.3 us (12%)
  starting transfers between devices  25.2 us (12%)
  waiting for transfers between devices  21.8 us (11%)
  other arithmetic  4.84 us (2%)
    pallas_call x4, Pallas kernels, column_sweep(): pl.pallas_call(functools.partial(column_kernel, sides), grid=(width // ti...  64.9 us
    pallas_call x3, Pallas kernels, row_sweep(): pl.pallas_call(functools.partial(row_kernel, count), grid=(rows // BLOCK,...  48 us
    ppermute x10, starting transfers between devices, exchange(): return (lax.ppermute(last, axis, up), lax.ppermute(first, axis, down))  25.2 us
    ppermute x10, waiting for transfers between devices, exchange(): return (lax.ppermute(last, axis, up), lax.ppermute(first, axis, down))  21.8 us
    slice x4, local copies, waits for them, and re-layouts, columns(): covariance[low:high, a * UNIT:b * UNIT]  14.6 us
    pallas_call x2, Pallas kernels, blocks_of(): pl.pallas_call(functools.partial(block_kernel, made, transposed), grid=(g...  12.8 us
    concatenate x3, other arithmetic, columns(): jnp.concatenate([covariance[low:high, a * UNIT:b * UNIT] for a, b in part...  4.84 us
    unnamed x22, local copies, waits for them, and re-layouts  4.19 us
  transfers between devices with their start and end apart: 10, of which 1 were waited for; matrix products, arithmetic and copies ran while one was open for 11% of the time, Pallas kernels for 56%

profile of v2, /device:TPU:6, one launch (start us, length us, event | category | flops | bytes accessed | tf_op | source)
XLA Modules:
  0.0 204.8 jit_solution(4052905336255704034)
XLA Ops:
  0.0 1.8 fusion
  1.8 1.2 pad_maximum_fusion.1
  2.9 1.9 collective-permute-start.4
  4.8 1.1 pad_maximum_fusion.2
  6.0 3.8 %collective-permute-start.5 = (f32[384,768]{1,0:T(8,128)}, f32[384,768]{1,0:T(8,128)}, u32[]{:S(2)}, u32[]{:S(2)}) collective-permute-start(f32[384,768]{1,0:T(8,128)} %pad_maximum_fusion.2), channel_id=1, source_target_pairs={{4,0},{8,4},{12,8},{16,12},{20,16},{24,20},{28,24},{5,1},{9,5},{13... | collective-permute-start | bytes 3538952 | tf_op jit(solution)/shard_map/ppermute | solution.py:196
  9.8 3.2 %fusion.2 = (f32[384,768]{1,0:T(8,128)}, f32[384,768]{1,0:T(8,128)}) fusion(f32[1536,3072]{1,0:T(8,128)} %refs_3_.5), kind=kLoop, calls=%fused_computation.5 | loop fusion | bytes 4718592 | tf_op jit(solution)/shard_map/slice | solution.py:225
  12.9 1.9 collective-permute-start.3
  14.8 0.0 copy-done.1
  14.9 0.0 copy-done.2
  14.9 0.0 copy-done.3
  14.9 0.0 copy-done.4
  14.9 1.9 shard_map.55
  16.8 1.3 copy-done
  18.1 4.2 %shard_map.56.refs_6_.refs_4_ = bf16[4,768,1152]{2,1,0:T(8,128)(2,1)} custom-call(s32[1]{0:T(128)} %bitcast.offset, f32[25,96,128]{2,1,0:T(8,128)S(1)} %copy-done), custom_call_target="tpu_custom_call" | custom-call | flops 10000000 | bytes 20000000 | tf_op jit(solution)/shard_map/pallas_call | solution.py:98
  22.3 25.2 %shard_map.61.refs_1_.refs_2_.refs_3_.refs_4_.refs_5_.refs_6_.refs_7_.refs_8_ = f32[768,3072]{1,0:T(8,128)} custom-call(f32[1536,3072]{1,0:T(8,128)} %refs_3_.5, f32[1536,3072]{1,0:T(8,128)} %refs_3_.5, f32[1536,3072]{1,0:T(8,128)} %refs_3_.5, f32[1536,3072]{1,0:T(8,128)} %refs_3_.5, bf16[4,768,1152]{2,1,0:T(8,128)(2,1)} %shard_map.56.refs_6_.refs_4_), custom_call_target="tpu_custom_call" | custom-call | flops 16307453952 | bytes 28311552 | tf_op jit(solution)/shard_map/pallas_call | solution.py:138
  47.5 3.2 %fusion.4 = (f32[768,384]{1,0:T(8,128)}, f32[768,384]{1,0:T(8,128)}) fusion(f32[768,3072]{1,0:T(8,128)} %shard_map.61.refs_1_.refs_2_.refs_3_.refs_4_.refs_5_.refs_6_.refs_7_.refs_8_), kind=kLoop, calls=%fused_computation.7 | loop fusion | bytes 4718592 | tf_op jit(solution)/shard_map/slice | solution.py:266
  50.7 1.3 collective-permute-start.9
  52.0 5.6 %collective-permute-start.8 = (f32[768,384]{1,0:T(8,128)}, f32[768,384]{1,0:T(8,128)}, u32[]{:S(2)}, u32[]{:S(2)}) collective-permute-start(f32[768,384]{1,0:T(8,128)} %get-tuple-element.20), channel_id=1, source_target_pairs={{0,1},{1,2},{2,3},{4,5},{5,6},{6,7},{8,9},{9,10},{10,11},{12,13},{... | collective-permute-start | bytes 3538952 | tf_op jit(solution)/shard_map/ppermute | solution.py:196
  57.6 4.9 %fusion.1 = (f32[1536,384]{1,0:T(8,128)}, f32[1536,384]{1,0:T(8,128)}) fusion(f32[1536,3072]{1,0:T(8,128)} %refs_3_.5), kind=kLoop, calls=%fused_computation.4 | loop fusion | bytes 9437184 | tf_op jit(solution)/shard_map/slice | solution.py:225
  62.5 4.9 %fusion.3 = (f32[384,1536]{1,0:T(8,128)}, f32[384,1536]{1,0:T(8,128)}) fusion(f32[1536,3072]{1,0:T(8,128)} %refs_3_.5), kind=kLoop, calls=%fused_computation.6 | loop fusion | bytes 9437184 | tf_op jit(solution)/shard_map/slice | solution.py:225
  67.3 8.6 %shard_map.60.refs_10_.refs_6_ = bf16[12,2048,256]{2,1,0:T(8,128)(2,1)} custom-call(s32[1]{0:T(128)} %bitcast.1.offset, f32[25,96,128]{2,1,0:T(8,128)S(1)} %get-tuple-element.8.table), custom_call_target="tpu_custom_call" | custom-call | flops 10000000 | bytes 20000000 | tf_op jit(solution)/shard_map/pallas_call | solution.py:98
  75.9 0.0 copy-done.5
  75.9 0.0 copy-done.6
  75.9 2.6 %pad_maximum_fusion.refs_1_.refs_2_.refs_3_.refs_4_ = f32[1536,768]{1,0:T(8,128)} fusion(f32[1536,384]{1,0:T(8,128)S(1)} %copy-done.6, f32[1536,384]{1,0:T(8,128)S(1)} %copy-done.5), kind=kLoop, calls=%fused_computation | loop fusion | flops 1179648 | bytes 9437184 | tf_op jit(solution)/shard_map/concatenate | solution.py:225
  78.4 0.0 collective-permute-done.4.refs_0_
  78.5 2.9 %collective-permute-start.1 = (f32[384,1536]{1,0:T(8,128)}, f32[384,1536]{1,0:T(8,128)S(1)}, u32[]{:S(2)}, u32[]{:S(2)}) collective-permute-start(f32[384,1536]{1,0:T(8,128)} %get-tuple-element.17), channel_id=1, source_target_pairs={{4,0},{8,4},{12,8},{16,12},{20,16},{24,20},{28,24},{5,1},{9,5},{13... | collective-permute-start | bytes 7077896 | tf_op jit(solution)/shard_map/ppermute | solution.py:196
  81.3 0.0 collective-permute-done.5.refs_5_
  81.4 1.9 collective-permute-start
  83.3 9.8 %shard_map.59.refs_1_.refs_4_ = f32[768,768]{1,0:T(8,128)} custom-call(f32[384,768]{1,0:T(8,128)S(1)} %collective-permute-done.4.refs_0_, f32[1536,768]{1,0:T(8,128)} %pad_maximum_fusion.refs_1_.refs_2_.refs_3_.refs_4_, f32[1536,768]{1,0:T(8,128)} %pad_maximum_fusion.refs_1_.refs_2_.refs_3_.refs_4_, ...), custom_call_target="tpu_custom_call" | custom-call | flops 4076863488 | bytes 7077888 | tf_op jit(solution)/shard_map/pallas_call | solution.py:138
  93.1 3.3 %fusion.5 = (f32[768,384]{1,0:T(8,128)}, f32[768,384]{1,0:T(8,128)}) fusion(f32[768,768]{1,0:T(8,128)} %shard_map.59.refs_1_.refs_4_), kind=kLoop, calls=%fused_computation.8 | loop fusion | bytes 4718592 | tf_op jit(solution)/shard_map/slice | solution.py:263
  96.3 0.0 collective-permute-done.9.refs_9_
  96.3 1.9 collective-permute-start.2
  98.2 0.0 collective-permute-done.8.refs_0_
  98.3 2.5 %collective-permute-start.7 = (f32[768,384]{1,0:T(8,128)}, f32[768,384]{1,0:T(8,128)S(1)}, u32[]{:S(2)}, u32[]{:S(2)}) collective-permute-start(f32[768,384]{1,0:T(8,128)} %get-tuple-element.21), channel_id=1, source_target_pairs={{0,1},{1,2},{2,3},{4,5},{5,6},{6,7},{8,9},{9,10},{10,11},{12,13},{... | collective-permute-start | bytes 3538952 | tf_op jit(solution)/shard_map/ppermute | solution.py:196
  100.8 22.8 %shard_map.62.refs_7_ = f32[1536,3072]{1,0:T(8,128)} custom-call(f32[768,384]{1,0:T(8,128)} %collective-permute-done.8.refs_0_, f32[768,3072]{1,0:T(8,128)} %shard_map.61.refs_1_.refs_2_.refs_3_.refs_4_.refs_5_.refs_6_.refs_7_.refs_8_, f32[768,3072]{1,0:T(8,128)} %shard_map.61.refs_1_.refs_2_.refs_3_.refs_4_.refs_5_.refs_6_.refs_7_.refs_8_, ...), custom_call_target="tpu_custom_call" | custom-call | flops 14495514624 | bytes 28311552 | tf_op jit(solution)/shard_map/pallas_call | solution.py:179
  123.6 0.0 collective-permute-done.3.refs_5_
  123.6 1.5 collective-permute-start.6
  125.1 21.7 %collective-permute-done.2.refs_0_ = f32[384,768]{1,0:T(8,128)S(1)} collective-permute-done((f32[384,768]{1,0:T(8,128)S(1)}, f32[384,768]{1,0:T(8,128)S(1)}, u32[]{:S(2)}, u32[]{:S(2)}) %collective-permute-start.2) | collective-permute-done | bytes 1179680 | tf_op jit(solution)/shard_map/ppermute | solution.py:196
  146.8 11.5 %shard_map.58.refs_2_.refs_3_ = f32[768,768]{1,0:T(8,128)} custom-call(f32[384,768]{1,0:T(8,128)S(1)} %collective-permute-done.2.refs_0_, f32[1536,3072]{1,0:T(8,128)} %refs_3_.5, f32[1536,3072]{1,0:T(8,128)} %refs_3_.5, f32[1536,3072]{1,0:T(8,128)} %refs_3_.5, f32[1536,3072]{1,0:T(8,128)} %refs_3_.5, f32[384,768]{1,0:T(8,128)} %collective-permute-done.3.refs_5_, ...), custom_call_target="tpu_custom_call" | custom-call | flops 4076863488 | bytes 7077888 | tf_op jit(solution)/shard_map/pallas_call | solution.py:138
  158.3 0.0 collective-permute-done.1.refs_5_
  158.3 0.0 collective-permute-done.refs_0_
  158.3 1.4 copy-done.7
  159.7 1.5 copy-done.8
  161.2 18.4 %shard_map.57.refs_2_.refs_3_.refs_4_.refs_5_.refs_0_.refs_1_ = f32[768,1536]{1,0:T(8,128)} custom-call(f32[384,1536]{1,0:T(8,128)} %copy-done.8, f32[1536,3072]{1,0:T(8,128)} %refs_3_.5, f32[1536,3072]{1,0:T(8,128)} %refs_3_.5, f32[1536,3072]{1,0:T(8,128)} %refs_3_.5, f32[1536,3072]{1,0:T(8,128)} %refs_3_.5, f32[384,1536]{1,0:T(8,128)} %copy-done.7, ...), custom_call_target="tpu_custom_call" | custom-call | flops 8153726976 | bytes 14155776 | tf_op jit(solution)/shard_map/pallas_call | solution.py:138
  179.6 0.0 collective-permute-done.7.refs_0_
  179.6 12.6 %shard_map.63.refs_7_ = f32[1536,3072]{1,0:T(8,128)} custom-call(f32[768,384]{1,0:T(8,128)S(1)} %collective-permute-done.7.refs_0_, f32[768,768]{1,0:T(8,128)} %shard_map.59.refs_1_.refs_4_, f32[768,1536]{1,0:T(8,128)} %shard_map.57.refs_2_.refs_3_.refs_4_.refs_5_.refs_0_.refs_1_, ...), custom_call_target="tpu_custom_call", output_to_operand_aliasing={{}: (7, {})} | custom-call | flops 7247757312 | bytes 14155776 | tf_op jit(solution)/shard_map/pallas_call | solution.py:179
  192.2 0.0 collective-permute-done.6.refs_5_
  192.2 12.6 %shard_map.64 = f32[1536,3072]{1,0:T(8,128)} custom-call(f32[768,1536]{1,0:T(8,128)} %shard_map.57.refs_2_.refs_3_.refs_4_.refs_5_.refs_0_.refs_1_, f32[768,1536]{1,0:T(8,128)} %shard_map.57.refs_2_.refs_3_.refs_4_.refs_5_.refs_0_.refs_1_, f32[768,768]{1,0:T(8,128)} %shard_map.58.refs_2_.refs_3_, ...), custom_call_target="tpu_custom_call", output_to_operand_aliasing={{}: (7, {})} | custom-call | flops 7247757312 | bytes 14155776 | tf_op jit(solution)/shard_map/pallas_call | solution.py:179
  (13 shorter events, 0.0 us)
Async XLA Ops:
  2.9 75.5 %collective-permute-start.4 = (f32[384,768]{1,0:T(8,128)}, f32[384,768]{1,0:T(8,128)S(1)}, u32[]{:S(2)}, u32[]{:S(2)}) collective-permute-start(f32[384,768]{1,0:T(8,128)} %pad_maximum_fusion.1), channel_id=1, source_target_pairs={{0,4},{4,8},{8,12},{12,16},{16,20},{20,24},{24,28},{1,5},{5,9},{9,... | collective-permute-start | bytes 3538952 | tf_op jit(solution)/shard_map/ppermute | solution.py:196
  6.0 8.9 %copy-start.1 = (f32[96,128]{1,0:T(8,128)S(1)}, f32[96,128]{1,0:T(8,128)}, u32[]{:S(2)}) copy-start(f32[96,128]{1,0:T(8,128)} %east_wind.1) | copy-start | bytes 147460
  6.0 8.9 %copy-start.2 = (f32[96,128]{1,0:T(8,128)S(1)}, f32[96,128]{1,0:T(8,128)}, u32[]{:S(2)}) copy-start(f32[96,128]{1,0:T(8,128)} %north_wind.1) | copy-start | bytes 147460
  6.0 8.9 %copy-start.3 = (f32[96,128]{1,0:T(8,128)S(1)}, f32[96,128]{1,0:T(8,128)}, u32[]{:S(2)}) copy-start(f32[96,128]{1,0:T(8,128)} %diffuse_lon.1) | copy-start | bytes 147460
  6.0 8.9 %copy-start.4 = (f32[96,128]{1,0:T(8,128)S(1)}, f32[96,128]{1,0:T(8,128)}, u32[]{:S(2)}) copy-start(f32[96,128]{1,0:T(8,128)} %diffuse_lat.1) | copy-start | bytes 147460
  6.0 75.4 %collective-permute-start.5 = (f32[384,768]{1,0:T(8,128)}, f32[384,768]{1,0:T(8,128)}, u32[]{:S(2)}, u32[]{:S(2)}) collective-permute-start(f32[384,768]{1,0:T(8,128)} %pad_maximum_fusion.2), channel_id=1, source_target_pairs={{4,0},{8,4},{12,8},{16,12},{20,16},{24,20},{28,24},{5,1},{9,5},{13... | collective-permute-start | bytes 3538952 | tf_op jit(solution)/shard_map/ppermute | solution.py:196
  12.9 110.7 %collective-permute-start.3 = (f32[384,768]{1,0:T(8,128)}, f32[384,768]{1,0:T(8,128)}, u32[]{:S(2)}, u32[]{:S(2)}) collective-permute-start(f32[384,768]{1,0:T(8,128)} %get-tuple-element.15), channel_id=1, source_target_pairs={{4,0},{8,4},{12,8},{16,12},{20,16},{24,20},{28,24},{5,1},{9,5},{13... | collective-permute-start | bytes 3538952 | tf_op jit(solution)/shard_map/ppermute | solution.py:196
  16.8 1.3 copy-start
  50.7 45.6 %collective-permute-start.9 = (f32[768,384]{1,0:T(8,128)}, f32[768,384]{1,0:T(8,128)}, u32[]{:S(2)}, u32[]{:S(2)}) collective-permute-start(f32[768,384]{1,0:T(8,128)} %get-tuple-element.19), channel_id=1, source_target_pairs={{1,0},{2,1},{3,2},{5,4},{6,5},{7,6},{9,8},{10,9},{11,10},{13,12},{... | collective-permute-start | bytes 3538952 | tf_op jit(solution)/shard_map/ppermute | solution.py:196
  52.0 46.2 %collective-permute-start.8 = (f32[768,384]{1,0:T(8,128)}, f32[768,384]{1,0:T(8,128)}, u32[]{:S(2)}, u32[]{:S(2)}) collective-permute-start(f32[768,384]{1,0:T(8,128)} %get-tuple-element.20), channel_id=1, source_target_pairs={{0,1},{1,2},{2,3},{4,5},{5,6},{6,7},{8,9},{9,10},{10,11},{12,13},{... | collective-permute-start | bytes 3538952 | tf_op jit(solution)/shard_map/ppermute | solution.py:196
  67.3 8.6 %copy-start.5 = (f32[1536,384]{1,0:T(8,128)S(1)}, f32[1536,384]{1,0:T(8,128)}, u32[]{:S(2)}) copy-start(f32[1536,384]{1,0:T(8,128)} %get-tuple-element.13) | copy-start | bytes 7077892
  67.3 8.6 %copy-start.6 = (f32[1536,384]{1,0:T(8,128)S(1)}, f32[1536,384]{1,0:T(8,128)}, u32[]{:S(2)}) copy-start(f32[1536,384]{1,0:T(8,128)} %get-tuple-element.14) | copy-start | bytes 7077892
  75.9 5.5 %copy-start.9 = (f32[384,1536]{1,0:T(8,128)S(1)}, f32[384,1536]{1,0:T(8,128)}, u32[]{:S(2)}) copy-start(f32[384,1536]{1,0:T(8,128)} %get-tuple-element.18) | copy-start | bytes 7077892
  78.5 79.8 %collective-permute-start.1 = (f32[384,1536]{1,0:T(8,128)}, f32[384,1536]{1,0:T(8,128)S(1)}, u32[]{:S(2)}, u32[]{:S(2)}) collective-permute-start(f32[384,1536]{1,0:T(8,128)} %get-tuple-element.17), channel_id=1, source_target_pairs={{4,0},{8,4},{12,8},{16,12},{20,16},{24,20},{28,24},{5,1},{9,5},{13... | collective-permute-start | bytes 7077896 | tf_op jit(solution)/shard_map/ppermute | solution.py:196
  81.4 76.9 %collective-permute-start = (f32[384,1536]{1,0:T(8,128)S(1)}, f32[384,1536]{1,0:T(8,128)S(1)}, u32[]{:S(2)}, u32[]{:S(2)}) collective-permute-start(f32[384,1536]{1,0:T(8,128)S(1)} %copy-done.9), channel_id=1, source_target_pairs={{0,4},{4,8},{8,12},{12,16},{16,20},{20,24},{24,28},{1,5},{5,9},{9,... | collective-permute-start | bytes 7077896 | tf_op jit(solution)/shard_map/ppermute | solution.py:196
  93.1 3.3 %copy-start.10 = (f32[384,768]{1,0:T(8,128)S(1)}, f32[384,768]{1,0:T(8,128)}, u32[]{:S(2)}) copy-start(f32[384,768]{1,0:T(8,128)} %get-tuple-element.16) | copy-start | bytes 3538948
  96.3 50.5 %collective-permute-start.2 = (f32[384,768]{1,0:T(8,128)S(1)}, f32[384,768]{1,0:T(8,128)S(1)}, u32[]{:S(2)}, u32[]{:S(2)}) collective-permute-start(f32[384,768]{1,0:T(8,128)S(1)} %copy-done.10), channel_id=1, source_target_pairs={{0,4},{4,8},{8,12},{12,16},{16,20},{20,24},{24,28},{1,5},{5,9},{9,... | collective-permute-start | bytes 3538952 | tf_op jit(solution)/shard_map/ppermute | solution.py:196
  98.3 81.3 %collective-permute-start.7 = (f32[768,384]{1,0:T(8,128)}, f32[768,384]{1,0:T(8,128)S(1)}, u32[]{:S(2)}, u32[]{:S(2)}) collective-permute-start(f32[768,384]{1,0:T(8,128)} %get-tuple-element.21), channel_id=1, source_target_pairs={{0,1},{1,2},{2,3},{4,5},{5,6},{6,7},{8,9},{9,10},{10,11},{12,13},{... | collective-permute-start | bytes 3538952 | tf_op jit(solution)/shard_map/ppermute | solution.py:196
  123.6 68.6 %collective-permute-start.6 = (f32[768,384]{1,0:T(8,128)}, f32[768,384]{1,0:T(8,128)S(1)}, u32[]{:S(2)}, u32[]{:S(2)}) collective-permute-start(f32[768,384]{1,0:T(8,128)} %get-tuple-element.22), channel_id=1, source_target_pairs={{1,0},{2,1},{3,2},{5,4},{6,5},{7,6},{9,8},{10,9},{11,10},{13,12},{... | collective-permute-start | bytes 3538952 | tf_op jit(solution)/shard_map/ppermute | solution.py:196
  158.3 1.4 copy-start.7
  159.7 1.5 copy-start.8

commit v3 on v2

--- a/solution.py
+++ b/solution.py
@@ -113,38 +113,60 @@
     return jnp.dot(a, b, preferred_element_type=jnp.float32)
 
 
-def column_kernel(sides, *refs):
-    ins, tables, out, high, low = refs[:-4], refs[-4], refs[-3], refs[-2], refs[-1]
-    for n, ref in enumerate(ins):
-        rows = slice(n * UNIT, (n + 1) * UNIT)
-        high[rows, :], low[rows, :] = split(ref[...])
-    for at, (start, group) in enumerate(sides):
-        rows = slice(start * UNIT, (start + 3) * UNIT)
-        both = dot(tables[group], high[rows, :])
-        other = dot(tables[group, :UNIT, :], low[rows, :])
-        out[at * UNIT : (at + 1) * UNIT, :] = both[:UNIT] + (both[UNIT:] + other)
-
-
-def column_sweep(arrays, sides, width, tables):
-    total = len(sides) * UNIT
-    tile = WIDE if all(n % WIDE == 0 for n in [width] + [c for _, _, c in arrays]) else UNIT
+def stencil(c, east, west, north, south, coef):
+    return coef[0] * c + coef[1] * east + coef[2] * west + coef[3] * north + coef[4] * south
+
+
+def column_kernel(parts, sides, *refs):
+    ins, tables, out = refs[: len(parts)], refs[len(parts)], refs[-1]
+    for side, (names, first, count) in enumerate(sides):
+
+        def source(line):
+            part, at = divmod(line, STEPS)
+            return ins[names[part]][at * NLON : (at + 1) * NLON, :]
+
+        lines = count + 2 * STEPS
+        got = {}
+        for line in range(lines):
+            got[0, line] = source(line)
+            for step in range(1, STEPS + 1):
+                mid = line - step
+                if mid < step:
+                    continue
+                c = got[step - 1, mid]
+                row = first + mid - 1
+                value = stencil(
+                    c,
+                    pltpu.roll(c, NLON - 1, 0),
+                    pltpu.roll(c, 1, 0),
+                    got[step - 1, mid + 1],
+                    got[step - 1, mid - 1],
+                    [tables[k, row] for k in range(5)],
+                )
+                got.pop((step - 1, mid - 1))
+                if step < STEPS:
+                    got[step, mid] = value
+                else:
+                    at = sum(s[2] for s in sides[:side]) + mid - STEPS
+                    out[at * NLON : (at + 1) * NLON, :] = value
+
+
+def column_sweep(arrays, sides, width, coefs):
+    total = sum(count for _, _, count in sides) * NLON
     in_specs = [
-        pl.BlockSpec((UNIT, tile), functools.partial(lambda i, r, c: (r, i + c), r=r, c=c // tile))
-        for _, r, c in arrays
+        pl.BlockSpec((UNIT, NLON), functools.partial(lambda i, r, c, skip: (r, jnp.where(i < UNIT // NLON, i + c, i + c + skip)), r=r, c=c, skip=skip)) for _, r, c, skip in arrays
     ]
-    in_specs.append(pl.BlockSpec(tables.shape, lambda i: (0, 0, 0), pipeline_mode=pl.Buffered(1)))
-    scratch = pltpu.VMEM((len(arrays) * UNIT, tile), jnp.bfloat16)
+    in_specs.append(pl.BlockSpec(coefs.shape, lambda i: (0, 0, 0, 0)))
     work = total * width
     return pl.pallas_call(
-        functools.partial(column_kernel, sides),
-        grid=(width // tile,),
+        functools.partial(column_kernel, arrays, sides),
+        grid=(width // NLON,),
         in_specs=in_specs,
-        out_specs=pl.BlockSpec((total, tile), lambda i: (0, i)),
+        out_specs=pl.BlockSpec((total, NLON), lambda i: (0, i)),
         out_shape=jax.ShapeDtypeStruct((total, width), jnp.float32),
-        scratch_shapes=[scratch, scratch],
         compiler_params=pltpu.CompilerParams(vmem_limit_bytes=VMEM),
-        cost_estimate=pl.CostEstimate(flops=work * 2 * 1152 * 3, bytes_accessed=work * 12, transcendentals=0),
-    )(*[a for a, _, _ in arrays], tables)
+        cost_estimate=pl.CostEstimate(flops=work * 40, bytes_accessed=work * 12, transcendentals=0),
+    )(*[a[0] for a in arrays], coefs)
 
 
 def row_kernel(count, *refs):
@@ -185,7 +207,7 @@
         input_output_aliases=aliases,
         scratch_shapes=[pltpu.VMEM((2 * BLOCK, len(arrays) * UNIT), jnp.bfloat16)],
         compiler_params=pltpu.CompilerParams(vmem_limit_bytes=VMEM),
-        cost_estimate=pl.CostEstimate(flops=work * 2 * 1024 * 3, bytes_accessed=work * 12, transcendentals=0),
+        cost_estimate=pl.CostEstimate(flops=work * 40, bytes_accessed=work * 12, transcendentals=0),
     )(*operands)
 
 
@@ -196,13 +218,30 @@
     return lax.ppermute(last, axis, up), lax.ppermute(first, axis, down)
 
 
+def coefficients(tables, offset, lines):
+    east_wind, north_wind, diffuse_lon, diffuse_lat = tables
+    made = jnp.stack(
+        [
+            1.0 - 2.0 * diffuse_lon - 2.0 * diffuse_lat,
+            diffuse_lon - 0.5 * east_wind,
+            diffuse_lon + 0.5 * east_wind,
+            diffuse_lat - 0.5 * north_wind,
+            diffuse_lat + 0.5 * north_wind,
+        ]
+    )
+    edge = STEPS - 1
+    made = jnp.pad(made, ((0, 0), (edge, edge), (0, 0)))
+    return lax.dynamic_slice_in_dim(made, offset, lines + 2 * edge, 1)
+
+
 def body(covariance, east_wind, north_wind, diffuse_lon, diffuse_lat):
     tables = (east_wind, north_wind, diffuse_lon, diffuse_lat)
     rows, cols = covariance.shape
     row_lines, col_lines = rows // NLON, cols // NLON
     row_units, col_units = rows // UNIT, cols // UNIT
-    plain, rolled = powers(tables)
-    row_tables = blocks_of(rolled, lax.axis_index("row") * row_lines, row_units, STEPS, False)
+    row_coefs = coefficients(tables, lax.axis_index("row") * row_lines, row_lines)
+    row_coefs = jnp.broadcast_to(row_coefs[:, :, :, None], row_coefs.shape + (NLON,))
+    plain, _ = powers(tables)
     col_tables = blocks_of(plain, lax.axis_index("col") * col_lines, col_lines // 2, 2, True)
 
     if col_units == 1:
@@ -229,28 +268,25 @@
     inner = None
     if row_units > 2:
         inner = column_sweep(
-            [(covariance, r, 0) for r in range(row_units)],
-            [(u, u + 1) for u in range(row_units - 2)],
+            [(covariance, r, 0, 0) for r in range(row_units)],
+            [(list(range(row_units)), STEPS, row_lines - 2 * STEPS)],
             cols,
-            row_tables,
+            row_coefs,
         )
 
     outer = []
     where = {}
     for k, (units, (before, after)) in enumerate(zip(pieces, halos)):
         width = len(units) * UNIT
-        if k == 0 and col_units > 1:
-            own = columns(units, 0, rows)
-            blocks = [(own, r, 0) for r in range(row_units)]
+        skip = (cols - 2 * UNIT) // NLON if k == 0 and col_units > 1 else 0
+        blocks = [(covariance, r, units[0] * (UNIT // NLON), skip) for r in range(row_units)]
+        if row_units == 1:
+            arrays = [(before, 0, 0, 0), blocks[0], (after, 0, 0, 0)]
+            sides = [([0, 1, 2], 0, STEPS)]
         else:
-            blocks = [(covariance, r, units[0] * UNIT) for r in range(row_units)]
-        if row_units == 1:
-            arrays = [(before, 0, 0), blocks[0], (after, 0, 0)]
-            sides = [(0, 0)]
-        else:
-            arrays = [(before, 0, 0), blocks[0], blocks[1], blocks[-2], blocks[-1], (after, 0, 0)]
-            sides = [(0, 0), (3, row_units - 1)]
-        outer.append(column_sweep(arrays, sides, width, row_tables))
+            arrays = [(before, 0, 0, 0), blocks[0], blocks[1], blocks[-2], blocks[-1], (after, 0, 0, 0)]
+            sides = [([0, 1, 2], 0, STEPS), ([3, 4, 5], row_lines - STEPS, STEPS)]
+        outer.append(column_sweep(arrays, sides, width, row_coefs))
         for at, u in enumerate(units):
             where[u] = (k, at)
 

time: 205 us -> 189 us (0.922)
  the two profiles are of different devices: /device:TPU:6 before, /device:TPU:27 now
where the time goes in v3:
time: 189 us; the launch traced here: 187 us
  Pallas kernels  126 us (67%)
  starting transfers between devices  27.8 us (15%)
  local copies, waits for them, and re-layouts  23.1 us (12%)
  waiting for transfers between devices  7.79 us (4%)
  other arithmetic  2.29 us (1%)
    pallas_call x4, Pallas kernels, column_sweep(): pl.pallas_call(functools.partial(column_kernel, arrays, sides), grid=(wid...  67.8 us
    pallas_call x3, Pallas kernels, row_sweep(): pl.pallas_call(functools.partial(row_kernel, count), grid=(rows // BLOCK,...  48 us
    ppermute x10, starting transfers between devices, exchange(): return (lax.ppermute(last, axis, up), lax.ppermute(first, axis, down))  27.8 us
    slice x3, local copies, waits for them, and re-layouts, columns(): covariance[low:high, a * UNIT:b * UNIT]  9.78 us
    pallas_call x1, Pallas kernels, blocks_of(): pl.pallas_call(functools.partial(block_kernel, made, transposed), grid=(g...  8.54 us
    ppermute x10, waiting for transfers between devices, exchange(): return (lax.ppermute(last, axis, up), lax.ppermute(first, axis, down))  7.79 us
    unnamed x18, local copies, waits for them, and re-layouts  4.22 us
  transfers between devices with their start and end apart: 10, of which 1 were waited for; matrix products, arithmetic and copies ran while one was open for 10% of the time, Pallas kernels for 61%

profile of v3, /device:TPU:27, one launch (start us, length us, event | category | flops | bytes accessed | tf_op | source)
XLA Modules:
  0.0 187.3 jit_solution(16058376735508066911)
XLA Ops:
  0.0 1.8 fusion
  1.8 1.1 pad_maximum_fusion
  2.9 3.7 %collective-permute-start.4 = (f32[384,768]{1,0:T(8,128)}, f32[384,768]{1,0:T(8,128)S(1)}, u32[]{:S(2)}, u32[]{:S(2)}) collective-permute-start(f32[384,768]{1,0:T(8,128)} %pad_maximum_fusion), channel_id=1, source_target_pairs={{0,4},{4,8},{8,12},{12,16},{16,20},{20,24},{24,28},{1,5},{5,9},{9,... | collective-permute-start | bytes 3538952 | tf_op jit(solution)/shard_map/ppermute | solution.py:218
  6.5 1.1 pad_maximum_fusion.1
  7.7 1.9 %collective-permute-start.5 = (f32[384,768]{1,0:T(8,128)}, f32[384,768]{1,0:T(8,128)}, u32[]{:S(2)}, u32[]{:S(2)}) collective-permute-start(f32[384,768]{1,0:T(8,128)} %pad_maximum_fusion.1), channel_id=1, source_target_pairs={{4,0},{8,4},{12,8},{16,12},{20,16},{24,20},{28,24},{5,1},{9,5},{13... | collective-permute-start | bytes 3538952 | tf_op jit(solution)/shard_map/ppermute | solution.py:218
  9.6 3.2 %fusion.1 = (f32[384,768]{1,0:T(8,128)}, f32[384,768]{1,0:T(8,128)}) fusion(f32[1536,3072]{1,0:T(8,128)} %refs_3_.7), kind=kLoop, calls=%fused_computation.9 | loop fusion | bytes 4718592 | tf_op jit(solution)/shard_map/slice | solution.py:264
  12.8 2.5 %collective-permute-start.3 = (f32[384,768]{1,0:T(8,128)}, f32[384,768]{1,0:T(8,128)}, u32[]{:S(2)}, u32[]{:S(2)}) collective-permute-start(f32[384,768]{1,0:T(8,128)} %get-tuple-element.11), channel_id=1, source_target_pairs={{4,0},{8,4},{12,8},{16,12},{20,16},{24,20},{28,24},{5,1},{9,5},{13... | collective-permute-start | bytes 3538952 | tf_op jit(solution)/shard_map/ppermute | solution.py:218
  15.4 0.0 copy-start
  15.4 0.0 copy-start.2
  15.4 0.0 copy-start.4
  15.4 0.0 copy-start.6
  15.4 4.0 %collective-permute-start.2 = (f32[384,768]{1,0:T(8,128)}, f32[384,768]{1,0:T(8,128)S(1)}, u32[]{:S(2)}, u32[]{:S(2)}) collective-permute-start(f32[384,768]{1,0:T(8,128)} %get-tuple-element.12), channel_id=1, source_target_pairs={{0,4},{4,8},{8,12},{12,16},{16,20},{20,24},{24,28},{1,5},{5,9},{9,... | collective-permute-start | bytes 3538952 | tf_op jit(solution)/shard_map/ppermute | solution.py:218
  19.5 4.8 %fusion.2 = (f32[384,1536]{1,0:T(8,128)}, f32[384,1536]{1,0:T(8,128)}) fusion(f32[1536,3072]{1,0:T(8,128)} %refs_3_.7), kind=kLoop, calls=%fused_computation.10 | loop fusion | bytes 9437184 | tf_op jit(solution)/shard_map/slice | solution.py:264
  24.3 1.9 %collective-permute-start.1 = (f32[384,1536]{1,0:T(8,128)}, f32[384,1536]{1,0:T(8,128)}, u32[]{:S(2)}, u32[]{:S(2)}) collective-permute-start(f32[384,1536]{1,0:T(8,128)} %get-tuple-element.13), channel_id=1, source_target_pairs={{4,0},{8,4},{12,8},{16,12},{20,16},{24,20},{28,24},{5,1},{9,5},{13... | collective-permute-start | bytes 7077896 | tf_op jit(solution)/shard_map/ppermute | solution.py:218
  26.3 0.0 copy-done.6
  26.3 3.1 %broadcast_in_dim.2.refs_6_.refs_4_ = f32[5,16,128,128]{3,2,1,0:T(8,128)} broadcast(f32[5,16,128]{2,1,0:T(8,128)S(1)} %pad_dynamic-slice_fusion), dimensions={0,1,2} | broadcast | bytes 5283840 | tf_op jit(solution)/shard_map/broadcast_in_dim | solution.py:243
  29.4 28.8 %shard_map.60.refs_1_.refs_2_.refs_3_.refs_4_.refs_5_.refs_6_.refs_7_.refs_8_ = f32[768,3072]{1,0:T(8,128)} custom-call(f32[1536,3072]{1,0:T(8,128)} %refs_3_.7, f32[1536,3072]{1,0:T(8,128)} %refs_3_.7, f32[1536,3072]{1,0:T(8,128)} %refs_3_.7, f32[1536,3072]{1,0:T(8,128)} %refs_3_.7, f32[5,16,128,128]{3,2,1,0:T(8,128)} %broadcast_in_dim.2.refs_6_.refs_4_), custom_call_target="tpu_custom_call" | custom-call | flops 94371840 | bytes 28311552 | tf_op jit(solution)/shard_map/pallas_call | solution.py:161
  58.2 0.0 collective-permute-done.4.refs_0_
  58.2 4.5 %collective-permute-start = (f32[384,1536]{1,0:T(8,128)}, f32[384,1536]{1,0:T(8,128)}, u32[]{:S(2)}, u32[]{:S(2)}) collective-permute-start(f32[384,1536]{1,0:T(8,128)} %get-tuple-element.14), channel_id=1, source_target_pairs={{0,4},{4,8},{8,12},{12,16},{16,20},{20,24},{24,28},{1,5},{5,9},{9,... | collective-permute-start | bytes 7077896 | tf_op jit(solution)/shard_map/ppermute | solution.py:218
  62.7 2.8 %fusion.3 = (f32[768,384]{1,0:T(8,128)S(1)}, f32[768,384]{1,0:T(8,128)}) fusion(f32[768,3072]{1,0:T(8,128)} %shard_map.60.refs_1_.refs_2_.refs_3_.refs_4_.refs_5_.refs_6_.refs_7_.refs_8_), kind=kLoop, calls=%fused_computation.11 | loop fusion | bytes 4718592 | tf_op jit(solution)/shard_map/slice | solution.py:302
  65.5 0.0 collective-permute-done.5.refs_5_
  65.5 2.1 %collective-permute-start.9 = (f32[768,384]{1,0:T(8,128)S(1)}, f32[768,384]{1,0:T(8,128)S(1)}, u32[]{:S(2)}, u32[]{:S(2)}) collective-permute-start(f32[768,384]{1,0:T(8,128)S(1)} %get-tuple-element.15), channel_id=1, source_target_pairs={{1,0},{2,1},{3,2},{5,4},{6,5},{7,6},{9,8},{10,9},{11,10},{13,12},{... | collective-permute-start | bytes 3538952 | tf_op jit(solution)/shard_map/ppermute | solution.py:218
  67.7 10.5 %shard_map.57.refs_1_.refs_4_ = f32[768,768]{1,0:T(8,128)} custom-call(f32[384,768]{1,0:T(8,128)S(1)} %collective-permute-done.4.refs_0_, f32[1536,3072]{1,0:T(8,128)} %refs_3_.7, f32[1536,3072]{1,0:T(8,128)} %refs_3_.7, f32[1536,3072]{1,0:T(8,128)} %refs_3_.7, f32[1536,3072]{1,0:T(8,128)} %refs_3_.7, f32[384,768]{1,0:T(8,128)} %collective-permute-done.5.refs_5_, ...), custom_call_target="tpu_custom_call" | custom-call | flops 23592960 | bytes 7077888 | tf_op jit(solution)/shard_map/pallas_call | solution.py:161
  78.2 0.0 collective-permute-done.3.refs_5_
  78.2 1.3 collective-permute-start.8
  79.5 3.2 %fusion.4 = (f32[768,384]{1,0:T(8,128)}, f32[768,384]{1,0:T(8,128)}) fusion(f32[768,768]{1,0:T(8,128)} %shard_map.57.refs_1_.refs_4_), kind=kLoop, calls=%fused_computation.12 | loop fusion | bytes 4718592 | tf_op jit(solution)/shard_map/slice | solution.py:299
  82.7 0.0 collective-permute-done.2.refs_0_
  82.7 1.3 collective-permute-start.7
  84.0 7.8 %collective-permute-done.9.refs_9_ = f32[768,384]{1,0:T(8,128)S(1)} collective-permute-done((f32[768,384]{1,0:T(8,128)S(1)}, f32[768,384]{1,0:T(8,128)S(1)}, u32[]{:S(2)}, u32[]{:S(2)}) %collective-permute-start.9) | collective-permute-done | bytes 1179680 | tf_op jit(solution)/shard_map/ppermute | solution.py:218
  91.7 1.0 copy-done.8
  92.7 4.5 %collective-permute-start.6 = (f32[768,384]{1,0:T(8,128)}, f32[768,384]{1,0:T(8,128)S(1)}, u32[]{:S(2)}, u32[]{:S(2)}) collective-permute-start(f32[768,384]{1,0:T(8,128)} %get-tuple-element.18), channel_id=1, source_target_pairs={{1,0},{2,1},{3,2},{5,4},{6,5},{7,6},{9,8},{10,9},{11,10},{13,12},{... | collective-permute-start | bytes 3538952 | tf_op jit(solution)/shard_map/ppermute | solution.py:218
  97.2 0.0 copy-start.1
  97.2 0.8 copy-done.1
  98.0 0.8 copy-done.3
  98.8 0.8 copy-done.5
  99.6 0.8 copy-done.7
  100.4 1.9 %shard_map.58 = (f32[25,96,128]{2,1,0:T(8,128)S(1)}, f32[25,96,128]{2,1,0:T(8,128)}) custom-call(f32[96,128]{1,0:T(8,128)S(1)} %copy-done.5, f32[96,128]{1,0:T(8,128)S(1)} %copy-done.7, f32[96,128]{1,0:T(8,128)S(1)} %copy-done.3, f32[96,128]{1,0:T(8,128)S(1)} %copy-done.1), custom_call_target="tpu_custom_call" | custom-call | flops 10000000 | bytes 10000000 | tf_op jit(solution)/shard_map/pallas_call | solution.py:58
  102.3 8.5 %shard_map.59.refs_10_.refs_6_ = bf16[12,2048,256]{2,1,0:T(8,128)(2,1)} custom-call(s32[1]{0:T(128)} %bitcast.5.offset, f32[25,96,128]{2,1,0:T(8,128)S(1)} %get-tuple-element.6.table), custom_call_target="tpu_custom_call" | custom-call | flops 10000000 | bytes 20000000 | tf_op jit(solution)/shard_map/pallas_call | solution.py:98
  110.8 10.4 %shard_map.56.refs_2_.refs_3_ = f32[768,768]{1,0:T(8,128)} custom-call(f32[384,768]{1,0:T(8,128)S(1)} %collective-permute-done.2.refs_0_, f32[1536,3072]{1,0:T(8,128)} %refs_3_.7, f32[1536,3072]{1,0:T(8,128)} %refs_3_.7, f32[1536,3072]{1,0:T(8,128)} %refs_3_.7, f32[1536,3072]{1,0:T(8,128)} %refs_3_.7, f32[384,768]{1,0:T(8,128)} %collective-permute-done.3.refs_5_, ...), custom_call_target="tpu_custom_call" | custom-call | flops 23592960 | bytes 7077888 | tf_op jit(solution)/shard_map/pallas_call | solution.py:161
  121.3 0.0 collective-permute-done.8.refs_0_
  121.3 22.8 %shard_map.61.refs_7_ = f32[1536,3072]{1,0:T(8,128)} custom-call(f32[768,384]{1,0:T(8,128)} %collective-permute-done.8.refs_0_, f32[768,3072]{1,0:T(8,128)} %shard_map.60.refs_1_.refs_2_.refs_3_.refs_4_.refs_5_.refs_6_.refs_7_.refs_8_, f32[768,3072]{1,0:T(8,128)} %shard_map.60.refs_1_.refs_2_.refs_3_.refs_4_.refs_5_.refs_6_.refs_7_.refs_8_, ...), custom_call_target="tpu_custom_call" | custom-call | flops 94371840 | bytes 28311552 | tf_op jit(solution)/shard_map/pallas_call | solution.py:201
  144.0 0.0 collective-permute-done.1.refs_5_
  144.0 0.0 collective-permute-done.refs_0_
  144.0 18.1 %shard_map.55.refs_2_.refs_3_.refs_4_.refs_5_.refs_0_.refs_1_ = f32[768,1536]{1,0:T(8,128)} custom-call(f32[384,1536]{1,0:T(8,128)} %collective-permute-done.refs_0_, f32[1536,3072]{1,0:T(8,128)} %refs_3_.7, f32[1536,3072]{1,0:T(8,128)} %refs_3_.7, f32[1536,3072]{1,0:T(8,128)} %refs_3_.7, f32[1536,3072]{1,0:T(8,128)} %refs_3_.7, ...), custom_call_target="tpu_custom_call" | custom-call | flops 47185920 | bytes 14155776 | tf_op jit(solution)/shard_map/pallas_call | solution.py:161
  162.1 0.0 collective-permute-done.7.refs_0_
  162.1 12.6 %shard_map.62.refs_7_ = f32[1536,3072]{1,0:T(8,128)} custom-call(f32[768,384]{1,0:T(8,128)S(1)} %collective-permute-done.7.refs_0_, f32[768,768]{1,0:T(8,128)} %shard_map.57.refs_1_.refs_4_, f32[768,1536]{1,0:T(8,128)} %shard_map.55.refs_2_.refs_3_.refs_4_.refs_5_.refs_0_.refs_1_, ...), custom_call_target="tpu_custom_call", output_to_operand_aliasing={{}: (7, {})} | custom-call | flops 47185920 | bytes 14155776 | tf_op jit(solution)/shard_map/pallas_call | solution.py:201
  174.7 0.0 collective-permute-done.6.refs_5_
  174.7 12.6 %shard_map.63 = f32[1536,3072]{1,0:T(8,128)} custom-call(f32[768,1536]{1,0:T(8,128)} %shard_map.55.refs_2_.refs_3_.refs_4_.refs_5_.refs_0_.refs_1_, f32[768,1536]{1,0:T(8,128)} %shard_map.55.refs_2_.refs_3_.refs_4_.refs_5_.refs_0_.refs_1_, f32[768,768]{1,0:T(8,128)} %shard_map.56.refs_2_.refs_3_, ...), custom_call_target="tpu_custom_call", output_to_operand_aliasing={{}: (7, {})} | custom-call | flops 47185920 | bytes 14155776 | tf_op jit(solution)/shard_map/pallas_call | solution.py:201
  (13 shorter events, 0.1 us)
Async XLA Ops:
  2.9 55.3 %collective-permute-start.4 = (f32[384,768]{1,0:T(8,128)}, f32[384,768]{1,0:T(8,128)S(1)}, u32[]{:S(2)}, u32[]{:S(2)}) collective-permute-start(f32[384,768]{1,0:T(8,128)} %pad_maximum_fusion), channel_id=1, source_target_pairs={{0,4},{4,8},{8,12},{12,16},{16,20},{20,24},{24,28},{1,5},{5,9},{9,... | collective-permute-start | bytes 3538952 | tf_op jit(solution)/shard_map/ppermute | solution.py:218
  7.7 57.9 %collective-permute-start.5 = (f32[384,768]{1,0:T(8,128)}, f32[384,768]{1,0:T(8,128)}, u32[]{:S(2)}, u32[]{:S(2)}) collective-permute-start(f32[384,768]{1,0:T(8,128)} %pad_maximum_fusion.1), channel_id=1, source_target_pairs={{4,0},{8,4},{12,8},{16,12},{20,16},{24,20},{28,24},{5,1},{9,5},{13... | collective-permute-start | bytes 3538952 | tf_op jit(solution)/shard_map/ppermute | solution.py:218
  12.8 65.4 %collective-permute-start.3 = (f32[384,768]{1,0:T(8,128)}, f32[384,768]{1,0:T(8,128)}, u32[]{:S(2)}, u32[]{:S(2)}) collective-permute-start(f32[384,768]{1,0:T(8,128)} %get-tuple-element.11), channel_id=1, source_target_pairs={{4,0},{8,4},{12,8},{16,12},{20,16},{24,20},{28,24},{5,1},{9,5},{13... | collective-permute-start | bytes 3538952 | tf_op jit(solution)/shard_map/ppermute | solution.py:218
  15.4 10.8 %copy-start = (f32[96,128]{1,0:T(8,128)S(1)}, f32[96,128]{1,0:T(8,128)}, u32[]{:S(2)}) copy-start(f32[96,128]{1,0:T(8,128)} %diffuse_lat.1) | copy-start | bytes 147460
  15.4 10.8 %copy-start.2 = (f32[96,128]{1,0:T(8,128)S(1)}, f32[96,128]{1,0:T(8,128)}, u32[]{:S(2)}) copy-start(f32[96,128]{1,0:T(8,128)} %diffuse_lon.1) | copy-start | bytes 147460
  15.4 10.8 %copy-start.4 = (f32[96,128]{1,0:T(8,128)S(1)}, f32[96,128]{1,0:T(8,128)}, u32[]{:S(2)}) copy-start(f32[96,128]{1,0:T(8,128)} %east_wind.1) | copy-start | bytes 147460
  15.4 10.9 %copy-start.6 = (f32[96,128]{1,0:T(8,128)S(1)}, f32[96,128]{1,0:T(8,128)}, u32[]{:S(2)}) copy-start(f32[96,128]{1,0:T(8,128)} %north_wind.1) | copy-start | bytes 147460
  15.4 67.3 %collective-permute-start.2 = (f32[384,768]{1,0:T(8,128)}, f32[384,768]{1,0:T(8,128)S(1)}, u32[]{:S(2)}, u32[]{:S(2)}) collective-permute-start(f32[384,768]{1,0:T(8,128)} %get-tuple-element.12), channel_id=1, source_target_pairs={{0,4},{4,8},{8,12},{12,16},{16,20},{20,24},{24,28},{1,5},{5,9},{9,... | collective-permute-start | bytes 3538952 | tf_op jit(solution)/shard_map/ppermute | solution.py:218
  24.3 119.8 %collective-permute-start.1 = (f32[384,1536]{1,0:T(8,128)}, f32[384,1536]{1,0:T(8,128)}, u32[]{:S(2)}, u32[]{:S(2)}) collective-permute-start(f32[384,1536]{1,0:T(8,128)} %get-tuple-element.13), channel_id=1, source_target_pairs={{4,0},{8,4},{12,8},{16,12},{20,16},{24,20},{28,24},{5,1},{9,5},{13... | collective-permute-start | bytes 7077896 | tf_op jit(solution)/shard_map/ppermute | solution.py:218
  58.2 85.8 %collective-permute-start = (f32[384,1536]{1,0:T(8,128)}, f32[384,1536]{1,0:T(8,128)}, u32[]{:S(2)}, u32[]{:S(2)}) collective-permute-start(f32[384,1536]{1,0:T(8,128)} %get-tuple-element.14), channel_id=1, source_target_pairs={{0,4},{4,8},{8,12},{12,16},{16,20},{20,24},{24,28},{1,5},{5,9},{9,... | collective-permute-start | bytes 7077896 | tf_op jit(solution)/shard_map/ppermute | solution.py:218
  65.5 26.2 %collective-permute-start.9 = (f32[768,384]{1,0:T(8,128)S(1)}, f32[768,384]{1,0:T(8,128)S(1)}, u32[]{:S(2)}, u32[]{:S(2)}) collective-permute-start(f32[768,384]{1,0:T(8,128)S(1)} %get-tuple-element.15), channel_id=1, source_target_pairs={{1,0},{2,1},{3,2},{5,4},{6,5},{7,6},{9,8},{10,9},{11,10},{13,12},{... | collective-permute-start | bytes 3538952 | tf_op jit(solution)/shard_map/ppermute | solution.py:218
  78.2 43.1 %collective-permute-start.8 = (f32[768,384]{1,0:T(8,128)}, f32[768,384]{1,0:T(8,128)}, u32[]{:S(2)}, u32[]{:S(2)}) collective-permute-start(f32[768,384]{1,0:T(8,128)} %get-tuple-element.16), channel_id=1, source_target_pairs={{0,1},{1,2},{2,3},{4,5},{5,6},{6,7},{8,9},{9,10},{10,11},{12,13},{... | collective-permute-start | bytes 3538952 | tf_op jit(solution)/shard_map/ppermute | solution.py:218
  82.7 79.5 %collective-permute-start.7 = (f32[768,384]{1,0:T(8,128)}, f32[768,384]{1,0:T(8,128)S(1)}, u32[]{:S(2)}, u32[]{:S(2)}) collective-permute-start(f32[768,384]{1,0:T(8,128)} %get-tuple-element.17), channel_id=1, source_target_pairs={{0,1},{1,2},{2,3},{4,5},{5,6},{6,7},{8,9},{9,10},{10,11},{12,13},{... | collective-permute-start | bytes 3538952 | tf_op jit(solution)/shard_map/ppermute | solution.py:218
  91.7 1.0 copy-start.8
  92.7 82.0 %collective-permute-start.6 = (f32[768,384]{1,0:T(8,128)}, f32[768,384]{1,0:T(8,128)S(1)}, u32[]{:S(2)}, u32[]{:S(2)}) collective-permute-start(f32[768,384]{1,0:T(8,128)} %get-tuple-element.18), channel_id=1, source_target_pairs={{1,0},{2,1},{3,2},{5,4},{6,5},{7,6},{9,8},{10,9},{11,10},{13,12},{... | collective-permute-start | bytes 3538952 | tf_op jit(solution)/shard_map/ppermute | solution.py:218
  97.2 0.8 copy-start.1
  98.0 0.8 copy-start.3
  98.8 0.8 copy-start.5
  99.6 0.8 copy-start.7
